TPU v7x, 32 devices: a whole 2x2x4 slice. The times are simulated.
32 devices in a mesh: dp: 4 (over y, x), seq: 8 (over z, core).
Axes of the slice: x: 2, y: 2, z: 4, core: 2. Of those that a mesh axis runs over, the one named last changes fastest.
Arguments:
- fine_rows: bfloat16 [4, 8192, 1536], P('dp', 'seq'), may hold values from -6 to 6
- queries: bfloat16 [4, 2048, 1536], P('dp', 'seq'), may hold values from -150 to 150
- value_weight: bfloat16 [1536, 1536], replicated, may hold values from -0.15625 to 0.15625
- block_lists: int32 [4, 32, 4], P('dp'), may hold values from -1 to 63, as said below
- out_grad: bfloat16 [4, 2048, 1536], P('dp', 'seq'), may hold values from -6 to 6
Outputs:
- attended: bfloat16 [4, 2048, 1536], P('dp', 'seq')
- query_grad: bfloat16 [4, 2048, 1536], P('dp', 'seq')
- row_grad: bfloat16 [4, 8192, 1536], P('dp', 'seq')
- weight_grad: float32 [1536, 1536], P('seq')
Inputs may be any that keep to these rules, and one draw needn't show every extreme that they name: `block_lists`: entries 0 to 1 of query block j are j * 2 to j * 2 + 1. Entry 2 + m (m from 0 to 1) of a query block on seq index r names one of the 8 blocks held by seq index r - (m + 1) * 2, or is -1 when that index is negative.
All inputs are finite; a program needn't handle non-finite values.
Results may differ from a plain program's by a relative error of at most 0.033.
Values may be sent and summed in bfloat16 or wider, within the bound.
A program may use at most 192 MiB of HBM per device.

v0:
```python
import math

import jax
import jax.numpy as jnp
from jax import lax
from jax.sharding import PartitionSpec as P

HEADS = 12
FBLK = 128
QBLK = 64
NSTR = 2


neg_big = -1e30


def shifted(block, axis, distance):
    devices = range(lax.axis_size(axis))
    route = [(i - distance, i) for i in devices if i - distance in devices]
    return lax.ppermute(block, axis, route)


def add_blocks(block_index, key_part, value_part, fine_count):
    flat_index = block_index.reshape(-1)
    block_hits = (jnp.arange(fine_count, dtype=jnp.int32)[:, None] == flat_index[None, :]).astype(
        jnp.bfloat16
    )
    model_width = key_part.shape[-1]
    key_rows = key_part.reshape(-1, FBLK, model_width)
    value_rows = value_part.reshape(-1, FBLK, model_width)
    key_add = jnp.einsum("fe,erw->frw", block_hits, key_rows, preferred_element_type=jnp.float32)
    value_add = jnp.einsum(
        "fe,erw->frw", block_hits, value_rows, preferred_element_type=jnp.float32
    )
    return (key_add, value_add)


def head_grads(
    query_heads, grad_heads, key_heads, value_heads, probs, probs_low, row_delta, score_scale
):
    dprob = jnp.einsum(
        "bqhd,bkhd->bhqk", grad_heads, value_heads, preferred_element_type=jnp.float32
    )
    dscore = (probs * (dprob - row_delta[..., None])).astype(jnp.bfloat16)
    query_part = (
        jnp.einsum("bhqk,bkhd->bqhd", dscore, key_heads, preferred_element_type=jnp.float32)
        * score_scale
    )
    key_part = (
        jnp.einsum("bhqk,bqhd->bkhd", dscore, query_heads, preferred_element_type=jnp.float32)
        * score_scale
    ).astype(jnp.bfloat16)
    value_part = jnp.einsum(
        "bhqk,bqhd->bkhd", probs_low, grad_heads, preferred_element_type=jnp.float32
    ).astype(jnp.bfloat16)
    return (query_part, key_part, value_part)


def delta_of(grad_heads, out_low):
    return jnp.sum(grad_heads.astype(jnp.float32) * out_low.astype(jnp.float32), axis=-1).transpose(
        0, 2, 1
    )


def served_blocks(list_rows, my_index, far_dist, column, query_count, fine_count):
    peer_rows = lax.dynamic_slice_in_dim(
        list_rows, (my_index + far_dist) * query_count, query_count, 0
    )
    return jnp.clip(peer_rows[:, column] - my_index * fine_count, 0, fine_count - 1)


def one_context(fine, query, value_weight, list_rows, out_cot):
    seq_count = lax.axis_size("seq")
    my_index = lax.axis_index("seq")
    row_count, model_width = fine.shape
    head_count = HEADS
    head_dim = model_width // head_count
    score_scale = 1.0 / math.sqrt(head_dim)
    fine_count = row_count // FBLK
    query_count = query.shape[0] // QBLK
    far_count = NSTR
    own_count = list_rows.shape[1] - far_count
    stride = seq_count // (far_count + 1)
    values = jnp.dot(fine, value_weight, preferred_element_type=jnp.float32).astype(jnp.bfloat16)
    fine_blocks = fine.reshape(fine_count, FBLK, model_width)
    value_blocks = values.reshape(fine_count, FBLK, model_width)
    my_lists = lax.dynamic_slice_in_dim(list_rows, my_index * query_count, query_count, 0)
    is_valid = my_lists >= 0
    own_index = my_lists[:, :own_count] - my_index * fine_count
    own_keys = jnp.take(fine_blocks, own_index, axis=0)
    own_values = jnp.take(value_blocks, own_index, axis=0)
    query_heads = query.reshape(query_count, QBLK, head_count, head_dim)
    grad_heads = out_cot.reshape(query_count, QBLK, head_count, head_dim)
    own_key_heads = own_keys.reshape(query_count, -1, head_count, head_dim)
    own_value_heads = own_values.reshape(query_count, -1, head_count, head_dim)
    own_scores = (
        jnp.einsum(
            "bqhd,bkhd->bhqk", query_heads, own_key_heads, preferred_element_type=jnp.float32
        )
        * score_scale
    )
    row_top = jnp.max(own_scores, axis=-1)
    served_list, far_tops, far_sums = ([], [], [])
    for far_step in range(far_count):
        far_dist = (far_step + 1) * stride
        block_index = served_blocks(
            list_rows, my_index, far_dist, own_count + far_step, query_count, fine_count
        )
        got_queries, got_grads = shifted((query_heads, grad_heads), "seq", -far_dist)
        block_keys = jnp.take(fine_blocks, block_index, axis=0).reshape(
            query_count, FBLK, head_count, head_dim
        )
        block_values = jnp.take(value_blocks, block_index, axis=0).reshape(
            query_count, FBLK, head_count, head_dim
        )
        far_scores = (
            jnp.einsum(
                "bqhd,bkhd->bhqk", got_queries, block_keys, preferred_element_type=jnp.float32
            )
            * score_scale
        )
        part_top = jnp.max(far_scores, axis=-1)
        part_total = jnp.sum(jnp.exp(far_scores - part_top[..., None]), axis=-1)
        got_top, got_total = shifted((part_top, part_total), "seq", far_dist)
        is_live = is_valid[:, own_count + far_step][:, None, None]
        far_tops.append(jnp.where(is_live, got_top, neg_big))
        far_sums.append(jnp.where(is_live, got_total, 0.0))
        served_list.append(
            (block_index, got_queries, got_grads, block_keys, block_values, far_scores)
        )
    for got_top in far_tops:
        row_top = jnp.maximum(row_top, got_top)
    row_total = jnp.sum(jnp.exp(own_scores - row_top[..., None]), axis=-1)
    for far_step in range(far_count):
        row_total = row_total + far_sums[far_step] * jnp.exp(far_tops[far_step] - row_top)
    own_probs = jnp.exp(own_scores - row_top[..., None]) / row_total[..., None]
    own_low = own_probs.astype(jnp.bfloat16)
    out_sum = jnp.einsum(
        "bhqk,bkhd->bqhd", own_low, own_value_heads, preferred_element_type=jnp.float32
    )
    owner_probs = []
    for far_step in range(far_count):
        far_dist = (far_step + 1) * stride
        block_index, got_queries, got_grads, block_keys, block_values, far_scores = served_list[
            far_step
        ]
        peer_top, peer_total = shifted((row_top, row_total), "seq", -far_dist)
        is_served = my_index + far_dist < seq_count
        far_probs = jnp.where(
            is_served, jnp.exp(far_scores - peer_top[..., None]) / peer_total[..., None], 0.0
        )
        far_low = far_probs.astype(jnp.bfloat16)
        part_out = jnp.einsum(
            "bhqk,bkhd->bqhd", far_low, block_values, preferred_element_type=jnp.float32
        )
        out_sum = out_sum + shifted(part_out.astype(jnp.bfloat16), "seq", far_dist).astype(
            part_out.dtype
        )
        owner_probs.append((far_probs, far_low))
    out_low = out_sum.astype(jnp.bfloat16)
    row_delta = delta_of(grad_heads, out_low)
    query_grad, key_part, value_part = head_grads(
        query_heads,
        grad_heads,
        own_key_heads,
        own_value_heads,
        own_probs,
        own_low,
        row_delta,
        score_scale,
    )
    key_sum, value_sum = add_blocks(
        own_index,
        key_part.reshape(query_count, own_count, FBLK, model_width),
        value_part.reshape(query_count, own_count, FBLK, model_width),
        fine_count,
    )
    for far_step in range(far_count):
        far_dist = (far_step + 1) * stride
        block_index, got_queries, got_grads, block_keys, block_values, far_scores = served_list[
            far_step
        ]
        far_probs, far_low = owner_probs[far_step]
        got_delta = shifted(row_delta, "seq", -far_dist)
        part_query, part_key, part_value = head_grads(
            got_queries,
            got_grads,
            block_keys,
            block_values,
            far_probs,
            far_low,
            got_delta,
            score_scale,
        )
        query_grad = query_grad + shifted(part_query, "seq", far_dist)
        key_add, value_add = add_blocks(
            block_index[:, None],
            part_key.reshape(query_count, 1, FBLK, model_width),
            part_value.reshape(query_count, 1, FBLK, model_width),
            fine_count,
        )
        key_sum = key_sum + key_add
        value_sum = value_sum + value_add
    value_total = value_sum.reshape(row_count, model_width).astype(jnp.bfloat16)
    back_rows = lax.dot_general(
        value_total, value_weight, (((1,), (1,)), ((), ())), preferred_element_type=jnp.float32
    )
    row_grad = (key_sum.reshape(row_count, model_width) + back_rows).astype(jnp.bfloat16)
    attended = out_low.reshape(-1, model_width)
    query_out = query_grad.astype(jnp.bfloat16).reshape(-1, model_width)
    return (attended, query_out, row_grad, value_total)


def shards(fine_rows, queries, value_weight, block_lists, out_grad):
    model_width = fine_rows.shape[2]
    pooled, query_grads, row_grads, value_totals = ([], [], [], [])
    attended, query_out, row_grad, value_total = one_context(
        fine_rows[0], queries[0], value_weight, block_lists[0], out_grad[0]
    )
    pooled.append(attended)
    query_grads.append(query_out)
    row_grads.append(row_grad)
    value_totals.append(value_total)
    fine_turned = fine_rows.reshape(-1, model_width).T
    value_all = value_totals[0]
    weight_share = lax.psum_scatter(
        jnp.dot(fine_turned, value_all, preferred_element_type=jnp.float32),
        "seq",
        scatter_dimension=0,
        tiled=True,
    )
    weight_grad = lax.psum(weight_share, "dp")
    return (jnp.stack(pooled), jnp.stack(query_grads), jnp.stack(row_grads), weight_grad)


def solution(mesh):
    return jax.shard_map(
        shards,
        mesh=mesh,
        in_specs=(
            P("dp", "seq", None),
            P("dp", "seq", None),
            P(),
            P("dp", None, None),
            P("dp", "seq", None),
        ),
        out_specs=(
            P("dp", "seq", None),
            P("dp", "seq", None),
            P("dp", "seq", None),
            P("seq", None),
        ),
        check_vma=False,
    )
```

profile of v0, /device:TPU:0, one launch (start us, length us, event | category | flops | bytes accessed | tf_op | source)
XLA Modules:
  0.0 534.6 jit_solution(2229375865626763262)
XLA Ops:
  15.4 8.7 %convolution_convert_fusion = bf16[1024,1536]{1,0:T(8,128)(2,1)} fusion(bf16[1536,1536]{1,0:T(8,128)(2,1)} %param.11, bf16[1,1024,1536]{2,1,0:T(8,128)(2,1)S(1)} %copy-done), kind=kOutput, calls=%fused_computation.12 | convolution fusion | flops 4833411072 | bytes 11010048 | tf_op jit(solution)/shard_map/dot_general | solution.py:84
  55.1 8.6 %copy.99 = bf16[4,2,128,1536]{2,1,3,0:T(2,128)(2,1)} copy(bf16[4,2,128,1536]{3,2,1,0:T(8,128)(2,1)} %get-tuple-element.32) | data formatting | bytes 6291456 | tf_op jit(solution)/shard_map/jit(_take)/select_n | solution.py:90
  63.7 6.0 %reshape.87 = bf16[4,256,12,128]{1,3,2,0:T(8,128)(2,1)} reshape(bf16[4,2,128,1536]{2,1,3,0:T(2,128)(2,1)} %copy.99) | data formatting | bytes 6291456 | tf_op jit(solution)/shard_map/reshape | solution.py:94
  78.0 7.7 %collective-permute-start.3 = (f32[4,12,64]{2,1,0:T(8,128)S(1)}, f32[4,12,64]{2,1,0:T(8,128)S(1)}, u32[]{:S(2)}, u32[]{:S(2)}) collective-permute-start(f32[4,12,64]{2,1,0:T(8,128)S(1)} %get-tuple-element.37), channel_id=1, source_target_pairs={{0,4},{1,5},{2,6},{3,7},{8,12},{9,13},{10,14},{11,15},{16,20},{17,... | collective-permute-start | bytes 36872 | tf_op jit(solution)/shard_map/ppermute | solution.py:20
  89.7 4.8 collective-permute-start.1
  113.9 7.8 %collective-permute-start.11 = (bf16[4,64,12,128]{3,1,2,0:T(8,128)(2,1)}, bf16[4,64,12,128]{3,1,2,0:T(8,128)(2,1)}, u32[]{:S(2)}, u32[]{:S(2)}) collective-permute-start(bf16[4,64,12,128]{3,1,2,0:T(8,128)(2,1)} %fusion.26), channel_id=1, source_target_pairs={{0,4},{1,5},{2,6},{3,7},{8,12},{9,13},{10,14},{11,15},{16,20},{17,... | collective-permute-start | bytes 2359304 | tf_op jit(solution)/shard_map/ppermute | solution.py:20
  123.8 4.8 collective-permute-start.8
  128.6 8.6 %copy.98 = bf16[4,2,128,1536]{2,1,3,0:T(2,128)(2,1)} copy(bf16[4,2,128,1536]{3,2,1,0:T(8,128)(2,1)} %get-tuple-element.31) | data formatting | bytes 6291456 | tf_op jit(solution)/shard_map/jit(_take)/select_n | solution.py:91
  137.3 6.0 %reshape.86 = bf16[4,256,12,128]{1,3,2,0:T(8,128)(2,1)} reshape(bf16[4,2,128,1536]{2,1,3,0:T(2,128)(2,1)} %copy.98) | data formatting | bytes 6291456 | tf_op jit(solution)/shard_map/reshape | solution.py:95
  145.6 7.5 %collective-permute-done.8 = bf16[4,64,12,128]{3,1,2,0:T(8,128)(2,1)} collective-permute-done((bf16[4,64,12,128]{3,1,2,0:T(8,128)(2,1)}, bf16[4,64,12,128]{3,1,2,0:T(8,128)(2,1)}, u32[]{:S(2)}, u32[]{:S(2)}) %collective-permute-start.8) | collective-permute-done | bytes 786464 | tf_op jit(solution)/shard_map/ppermute | solution.py:20
  161.4 5.0 convert_bitcast_fusion
  166.4 6.1 %copy.134 = bf16[4,256,12,128]{1,0,3,2:T(4,128)(2,1)} copy(bf16[4,256,12,128]{3,1,2,0:T(8,128)(2,1)} %convert_bitcast_fusion) | data formatting | bytes 6291456 | tf_op jit(solution)/shard_map/convert_element_type | solution.py:55
  172.5 5.8 %reshape_reshape.21 = bf16[8,128,1536]{1,0,2:T(8,128)(2,1)} reshape(bf16[4,256,12,128]{1,0,3,2:T(4,128)(2,1)} %copy.134) | data formatting | bytes 6291456 | tf_op jit(solution)/shard_map/reshape;reshape | solution.py:30
  178.3 5.5 %copy.135 = bf16[8,128,1536]{2,0,1:T(8,128)(2,1)} copy(bf16[8,128,1536]{1,0,2:T(8,128)(2,1)} %reshape_reshape.21) | data formatting | bytes 6291456 | tf_op jit(solution)/shard_map/reshape;reshape | solution.py:30
  183.7 5.6 %fusion.34 = f32[8,128,1536]{2,0,1:T(8,128)} fusion(bf16[8,128,1536]{2,0,1:T(8,128)(2,1)} %copy.135, s32[8]{0:T(128)S(1)} %eq.42), kind=kOutput, calls=%fused_computation.84 | convolution fusion | flops 25165888 | bytes 9437216 | tf_op jit(solution)/shard_map/fe,erw->frw/dot_general | solution.py:32
  189.4 10.8 %collective-permute-done.12 = bf16[4,64,12,128]{3,1,2,0:T(8,128)(2,1)} collective-permute-done((bf16[4,64,12,128]{3,1,2,0:T(8,128)(2,1)}, bf16[4,64,12,128]{3,1,2,0:T(8,128)(2,1)}, u32[]{:S(2)}, u32[]{:S(2)}) %collective-permute-start.12) | collective-permute-done | bytes 786464 | tf_op jit(solution)/shard_map/ppermute | solution.py:20
  223.5 6.0 %add_convert_fusion = bf16[8,128,1536]{2,0,1:T(8,128)(2,1)S(1)} fusion(f32[8,128,1536]{2,0,1:T(8,128)} %fusion.34, f32[8,128,1536]{2,0,1:T(8,128)} %fusion.44, bf16[4,128,1536]{2,0,1:T(4,128)(2,1)} %copy.137, s32[4]{0:T(128)S(1)} %clamp_reduce_fusion), kind=kOutput, calls=%fused_computation.9 | convolution fusion | flops 17301536 | bytes 17301520 | tf_op jit(solution)/shard_map/fe,erw->frw/dot_general | solution.py:32
  232.1 7.6 %convolution_bitcast_fusion = f32[1536,1536]{0,1:T(8,128)} fusion(bf16[1024,1536]{1,0:T(8,128)(2,1)S(1)} %bitcast.213, bf16[1,1024,1536]{2,1,0:T(8,128)(2,1)S(1)} %copy-done), kind=kOutput, calls=%fused_computation.6 | convolution fusion | flops 4831838208 | bytes 15728640 | tf_op jit(solution)/shard_map/dot_general | solution.py:227
  239.7 9.6 %copy.152 = f32[1536,1536]{1,0:T(8,128)} copy(f32[1536,1536]{0,1:T(8,128)} %convolution_bitcast_fusion) | data formatting | bytes 18874368
  286.6 32.8 %collective-permute-start.17 = (f32[4,64,12,128]{3,1,2,0:T(8,128)}, f32[4,64,12,128]{3,1,2,0:T(8,128)}, u32[]{:S(2)}, u32[]{:S(2)}) collective-permute-start(f32[4,64,12,128]{3,1,2,0:T(8,128)} %multiply_bitcast_fusion), channel_id=1, source_target_pairs={{0,4},{1,5},{2,6},{3,7},{8,12},{9,13},{10,14},{11,15},{16,20},{17,... | collective-permute-start | bytes 4718600 | tf_op jit(solution)/shard_map/ppermute | solution.py:20
  343.2 6.3 %copy.132 = f32[8,128,1536]{2,1,0:T(8,128)} copy(f32[8,128,1536]{2,0,1:T(8,128)S(1)} %add_add_fusion) | data formatting | bytes 12582912 | tf_op jit(solution)/shard_map/add | solution.py:202
  349.5 76.5 %reduce-scatter.4.cloned.1.call-done = f32[192,1536]{1,0:T(8,128)} async-done(((f32[1536,1536]{1,0:T(8,128)}), f32[192,1536]{1,0:T(8,128)}) %reduce-scatter.4.cloned.1.call-update) | async-done | bytes 1179664
  429.0 10.4 %fusion.1 = bf16[1,1024,1536]{2,1,0:T(8,128)(2,1)} fusion(bf16[1024,1536]{1,0:T(8,128)(2,1)} %bitcast.214, bf16[1536,1536]{1,0:T(8,128)(2,1)} %param.11, f32[8,128,1536]{2,1,0:T(8,128)} %copy.132), kind=kOutput, calls=%fused_computation.13 | convolution fusion | flops 4834983936 | bytes 17301504 | tf_op jit(solution)/shard_map/dot_general | solution.py:205
  446.5 77.9 %all-reduce.2.cloned.1.call-done = f32[192,1536]{0,1:T(8,128)} async-done(((f32[192,1536]{0,1:T(8,128)}), f32[192,1536]{0,1:T(8,128)}) %all-reduce.2.cloned.1.call-update) | async-done | bytes 1179664 | tf_op jit(solution)/shard_map/psum | solution.py:232
  (169 shorter events, 183.0 us)
Async XLA Ops:
  7.2 418.9 %reduce-scatter.4.cloned.1.call-start = ((), (), s32[]{:S(2)}) async-start(), calls=%async_computation.2 | async-start | bytes 10616832
  12.1 63.5 %collective-permute-start.2 = (bf16[4,64,12,128]{3,1,2,0:T(8,128)(2,1)}, bf16[4,64,12,128]{3,1,2,0:T(8,128)(2,1)}, u32[]{:S(2)}, u32[]{:S(2)}) collective-permute-start(bf16[4,64,12,128]{3,1,2,0:T(8,128)(2,1)} %copy.101), channel_id=1, source_target_pairs={{4,0},{5,1},{6,2},{7,3},{12,8},{13,9},{14,10},{15,11},{20,16},{21,... | collective-permute-start | bytes 2359304 | tf_op jit(solution)/shard_map/ppermute | solution.py:20
  13.4 74.6 %collective-permute-start = (bf16[4,64,12,128]{3,1,2,0:T(8,128)(2,1)}, bf16[4,64,12,128]{3,1,2,0:T(8,128)(2,1)}, u32[]{:S(2)}, u32[]{:S(2)}) collective-permute-start(bf16[4,64,12,128]{3,1,2,0:T(8,128)(2,1)} %copy.101), channel_id=1, source_target_pairs={{2,0},{3,1},{4,2},{5,3},{6,4},{7,5},{10,8},{11,9},{12,10},{13,11},... | collective-permute-start | bytes 2359304 | tf_op jit(solution)/shard_map/ppermute | solution.py:20
  78.0 19.5 %collective-permute-start.3 = (f32[4,12,64]{2,1,0:T(8,128)S(1)}, f32[4,12,64]{2,1,0:T(8,128)S(1)}, u32[]{:S(2)}, u32[]{:S(2)}) collective-permute-start(f32[4,12,64]{2,1,0:T(8,128)S(1)} %get-tuple-element.37), channel_id=1, source_target_pairs={{0,4},{1,5},{2,6},{3,7},{8,12},{9,13},{10,14},{11,15},{16,20},{17,... | collective-permute-start | bytes 36872 | tf_op jit(solution)/shard_map/ppermute | solution.py:20
  86.6 12.0 %collective-permute-start.5 = (f32[4,12,64]{2,1,0:T(8,128)S(1)}, f32[4,12,64]{2,1,0:T(8,128)S(1)}, u32[]{:S(2)}, u32[]{:S(2)}) collective-permute-start(f32[4,12,64]{2,1,0:T(8,128)S(1)} %fusion.16), channel_id=1, source_target_pairs={{0,4},{1,5},{2,6},{3,7},{8,12},{9,13},{10,14},{11,15},{16,20},{17,... | collective-permute-start | bytes 36872 | tf_op jit(solution)/shard_map/ppermute | solution.py:20
  89.7 7.7 %collective-permute-start.1 = (f32[4,12,64]{2,1,0:T(8,128)S(1)}, f32[4,12,64]{2,1,0:T(8,128)S(1)}, u32[]{:S(2)}, u32[]{:S(2)}) collective-permute-start(f32[4,12,64]{2,1,0:T(8,128)S(1)} %get-tuple-element.41), channel_id=1, source_target_pairs={{0,2},{1,3},{2,4},{3,5},{4,6},{5,7},{8,10},{9,11},{10,12},{11,13},... | collective-permute-start | bytes 36872 | tf_op jit(solution)/shard_map/ppermute | solution.py:20
  95.5 3.5 collective-permute-start.4
  99.1 10.8 %collective-permute-start.10 = (f32[4,12,64]{2,1,0:T(8,128)S(1)}, f32[4,12,64]{2,1,0:T(8,128)S(1)}, u32[]{:S(2)}, u32[]{:S(2)}) collective-permute-start(f32[4,12,64]{2,1,0:T(8,128)S(1)} %multiply_add_fusion), channel_id=1, source_target_pairs={{4,0},{5,1},{6,2},{7,3},{12,8},{13,9},{14,10},{15,11},{20,16},{21,... | collective-permute-start | bytes 36872 | tf_op jit(solution)/shard_map/ppermute | solution.py:20
  100.4 9.5 %collective-permute-start.9 = (f32[4,12,64]{2,1,0:T(8,128)S(1)}, f32[4,12,64]{2,1,0:T(8,128)S(1)}, u32[]{:S(2)}, u32[]{:S(2)}) collective-permute-start(f32[4,12,64]{2,1,0:T(8,128)S(1)} %maximum_maximum_fusion), channel_id=1, source_target_pairs={{4,0},{5,1},{6,2},{7,3},{12,8},{13,9},{14,10},{15,11},{20,16},{21,... | collective-permute-start | bytes 36872 | tf_op jit(solution)/shard_map/ppermute | solution.py:20
  107.3 14.4 %collective-permute-start.7 = (f32[4,12,64]{2,1,0:T(8,128)S(1)}, f32[4,12,64]{2,1,0:T(8,128)S(1)}, u32[]{:S(2)}, u32[]{:S(2)}) collective-permute-start(f32[4,12,64]{2,1,0:T(8,128)S(1)} %multiply_add_fusion), channel_id=1, source_target_pairs={{2,0},{3,1},{4,2},{5,3},{6,4},{7,5},{10,8},{11,9},{12,10},{13,11},... | collective-permute-start | bytes 36872 | tf_op jit(solution)/shard_map/ppermute | solution.py:20
  108.6 13.1 %collective-permute-start.6 = (f32[4,12,64]{2,1,0:T(8,128)S(1)}, f32[4,12,64]{2,1,0:T(8,128)S(1)}, u32[]{:S(2)}, u32[]{:S(2)}) collective-permute-start(f32[4,12,64]{2,1,0:T(8,128)S(1)} %maximum_maximum_fusion), channel_id=1, source_target_pairs={{2,0},{3,1},{4,2},{5,3},{6,4},{7,5},{10,8},{11,9},{12,10},{13,11},... | collective-permute-start | bytes 36872 | tf_op jit(solution)/shard_map/ppermute | solution.py:20
  113.9 31.7 %collective-permute-start.11 = (bf16[4,64,12,128]{3,1,2,0:T(8,128)(2,1)}, bf16[4,64,12,128]{3,1,2,0:T(8,128)(2,1)}, u32[]{:S(2)}, u32[]{:S(2)}) collective-permute-start(bf16[4,64,12,128]{3,1,2,0:T(8,128)(2,1)} %fusion.26), channel_id=1, source_target_pairs={{0,4},{1,5},{2,6},{3,7},{8,12},{9,13},{10,14},{11,15},{16,20},{17,... | collective-permute-start | bytes 2359304 | tf_op jit(solution)/shard_map/ppermute | solution.py:20
  123.8 29.4 %collective-permute-start.8 = (bf16[4,64,12,128]{3,1,2,0:T(8,128)(2,1)}, bf16[4,64,12,128]{3,1,2,0:T(8,128)(2,1)}, u32[]{:S(2)}, u32[]{:S(2)}) collective-permute-start(bf16[4,64,12,128]{3,1,2,0:T(8,128)(2,1)} %fusion.25), channel_id=1, source_target_pairs={{0,2},{1,3},{2,4},{3,5},{4,6},{5,7},{8,10},{9,11},{10,12},{11,13},... | collective-permute-start | bytes 2359304 | tf_op jit(solution)/shard_map/ppermute | solution.py:20
  158.8 57.0 %collective-permute-start.15 = (bf16[4,64,12,128]{3,1,2,0:T(8,128)(2,1)}, bf16[4,64,12,128]{3,1,2,0:T(8,128)(2,1)}, u32[]{:S(2)}, u32[]{:S(2)}) collective-permute-start(bf16[4,64,12,128]{3,1,2,0:T(8,128)(2,1)} %get-tuple-element.25), channel_id=1, source_target_pairs={{4,0},{5,1},{6,2},{7,3},{12,8},{13,9},{14,10},{15,11},{20,16},{21,... | collective-permute-start | bytes 2359304 | tf_op jit(solution)/shard_map/ppermute | solution.py:20
  160.1 40.0 %collective-permute-start.12 = (bf16[4,64,12,128]{3,1,2,0:T(8,128)(2,1)}, bf16[4,64,12,128]{3,1,2,0:T(8,128)(2,1)}, u32[]{:S(2)}, u32[]{:S(2)}) collective-permute-start(bf16[4,64,12,128]{3,1,2,0:T(8,128)(2,1)} %get-tuple-element.25), channel_id=1, source_target_pairs={{2,0},{3,1},{4,2},{5,3},{6,4},{7,5},{10,8},{11,9},{12,10},{13,11},... | collective-permute-start | bytes 2359304 | tf_op jit(solution)/shard_map/ppermute | solution.py:20
  249.4 275.0 %all-reduce.2.cloned.1.call-start = ((), (), s32[]{:S(2)}) async-start(), calls=%async_computation.1 | async-start | bytes 3145728 | tf_op jit(solution)/shard_map/psum | solution.py:232
  249.4 31.7 %collective-permute-start.16 = (f32[4,12,64]{2,1,0:T(8,128)S(1)}, f32[4,12,64]{2,1,0:T(8,128)S(1)}, u32[]{:S(2)}, u32[]{:S(2)}) collective-permute-start(f32[4,12,64]{2,1,0:T(8,128)S(1)} %bitcast.221), channel_id=1, source_target_pairs={{4,0},{5,1},{6,2},{7,3},{12,8},{13,9},{14,10},{15,11},{20,16},{21,... | collective-permute-start | bytes 36872 | tf_op jit(solution)/shard_map/ppermute | solution.py:20
  251.0 68.4 %collective-permute-start.13 = (f32[4,12,64]{2,1,0:T(8,128)S(1)}, f32[4,12,64]{2,1,0:T(8,128)S(1)}, u32[]{:S(2)}, u32[]{:S(2)}) collective-permute-start(f32[4,12,64]{2,1,0:T(8,128)S(1)} %bitcast.222), channel_id=1, source_target_pairs={{2,0},{3,1},{4,2},{5,3},{6,4},{7,5},{10,8},{11,9},{12,10},{13,11},... | collective-permute-start | bytes 36872 | tf_op jit(solution)/shard_map/ppermute | solution.py:20
  284.2 35.2 %copy-start.15 = (f32[4,12,128,64]{2,3,1,0:T(8,128)S(1)}, f32[4,12,128,64]{2,3,1,0:T(8,128)}, u32[]{:S(2)}) copy-start(f32[4,12,128,64]{2,3,1,0:T(8,128)} %copy-done.12) | copy-start | bytes 4718596
  284.2 35.2 %copy-start.29 = (bf16[4,128,1536]{1,2,0:T(8,128)(2,1)S(1)}, bf16[4,128,1536]{1,2,0:T(8,128)(2,1)}, u32[]{:S(2)}) copy-start(bf16[4,128,1536]{1,2,0:T(8,128)(2,1)} %copy.111) | copy-start | bytes 4718596
  286.5 35.3 %copy-start.7 = (bf16[4,128,1536]{1,2,0:T(8,128)(2,1)S(1)}, bf16[4,128,1536]{1,2,0:T(8,128)(2,1)}, u32[]{:S(2)}) copy-start(bf16[4,128,1536]{1,2,0:T(8,128)(2,1)} %copy.103) | copy-start | bytes 4718596
  286.6 152.8 %collective-permute-start.17 = (f32[4,64,12,128]{3,1,2,0:T(8,128)}, f32[4,64,12,128]{3,1,2,0:T(8,128)}, u32[]{:S(2)}, u32[]{:S(2)}) collective-permute-start(f32[4,64,12,128]{3,1,2,0:T(8,128)} %multiply_bitcast_fusion), channel_id=1, source_target_pairs={{0,4},{1,5},{2,6},{3,7},{8,12},{9,13},{10,14},{11,15},{16,20},{17,... | collective-permute-start | bytes 4718600 | tf_op jit(solution)/shard_map/ppermute | solution.py:20
  324.2 115.1 %collective-permute-start.14 = (f32[4,64,12,128]{3,1,2,0:T(8,128)}, f32[4,64,12,128]{3,1,2,0:T(8,128)}, u32[]{:S(2)}, u32[]{:S(2)}) collective-permute-start(f32[4,64,12,128]{3,1,2,0:T(8,128)} %multiply_bitcast_fusion.1), channel_id=1, source_target_pairs={{0,2},{1,3},{2,4},{3,5},{4,6},{5,7},{8,10},{9,11},{10,12},{11,13},... | collective-permute-start | bytes 4718600 | tf_op jit(solution)/shard_map/ppermute | solution.py:20
  444.0 83.3 %copy-start.1 = (bf16[1,1024,1536]{2,1,0:T(8,128)(2,1)S(1)}, bf16[1,1024,1536]{2,1,0:T(8,128)(2,1)}, u32[]{:S(2)}) copy-start(bf16[1,1024,1536]{2,1,0:T(8,128)(2,1)} %param.9) | copy-start | bytes 9437188
  (27 other events, 194.1 us)
Sparse Core Ops, SparseCore 0:
  249.5 176.4 reduce-scatter.3
  429.1 95.2 all-reduce.1
where the time goes:
time: 545 us; the launch traced here: 535 us
  waiting for transfers between devices  178 us (33%)
  local copies, waits for them, and re-layouts  139 us (26%)
  matrix products  108 us (20%)
  starting transfers between devices  79.4 us (15%)
  between operations  15.2 us (3%)
  other arithmetic  14.2 us (3%)
    ppermute x18, starting transfers between devices, shifted(): return lax.ppermute(block, axis, route)  79.3 us
    psum x1, waiting for transfers between devices, shards(): weight_grad = lax.psum(weight_share, 'dp')  77.9 us
    unnamed x3, waiting for transfers between devices  76.6 us
    ppermute x18, waiting for transfers between devices, shifted(): return lax.ppermute(block, axis, route)  24 us
    unnamed x65, local copies, waits for them, and re-layouts  19.2 us
    another operation x4, local copies, waits for them, and re-layouts, add_blocks(): value_rows = value_part.reshape(-1, FBLK, model_width)  19.1 us
    dot_general x3, matrix products, add_blocks(): jnp.einsum('fe,erw->frw', block_hits, value_rows, preferred_element_type=...  16.3 us
    dot_general x3, matrix products, head_grads(): jnp.einsum('bhqk,bqhd->bkhd', probs_low, grad_heads, preferred_element_ty...  12.5 us
  transfers between devices with their start and end apart: 20, of which 7 were waited for; matrix products, arithmetic and copies ran while one was open for 40% of the time, Pallas kernels for 0%

commit v1 on v0

v1 whole, which is shorter than its diff:
```python
import functools
import math

import jax
import jax.numpy as jnp
from jax import lax
from jax.experimental import pallas as pl
from jax.experimental.pallas import tpu as pltpu
from jax.sharding import PartitionSpec as P

HEADS = 12
FBLK = 128
QBLK = 64
NSTR = 2
DELTA_LANE = 64

neg_big = -1e30


def shifted(block, distance):
    devices = range(lax.axis_size("seq"))
    route = [(i - distance, i) for i in devices if i - distance in devices]
    return lax.ppermute(block, "seq", route)


def rows_by_rows(a, b):
    return lax.dot_general(a, b, (((1,), (1,)), ((), ())), preferred_element_type=jnp.float32)


def turned(a, b):
    return lax.dot_general(a, b, (((0,), (0,)), ((), ())), preferred_element_type=jnp.float32)


def plain(a, b):
    return jnp.dot(a, b, preferred_element_type=jnp.float32)


def head_slices(width):
    size = width // HEADS
    return [slice(h * size, (h + 1) * size) for h in range(HEADS)]


def attend_head(q, k, v, scale):
    scores = rows_by_rows(q, k) * scale
    top = jnp.max(scores, axis=-1, keepdims=True)
    raised = jnp.exp(scores - top)
    total = jnp.sum(raised, axis=-1, keepdims=True)
    out = plain(raised.astype(jnp.bfloat16), v) / total
    return out, top + jnp.log(total)


def merged(out_a, log_a, out_b, log_b):
    top = jnp.maximum(log_a, log_b)
    a = jnp.exp(log_a - top)
    b = jnp.exp(log_b - top)
    total = a + b
    return (out_a * a + out_b * b) / total, top + jnp.log(total)


def lanes(rows):
    return lax.broadcasted_iota(jnp.int32, (rows, 128), 1)


def far_first_kernel(index_ref, q_ref, k_ref, v_ref, out_ref, stat_ref, *, scale):
    lane = lanes(q_ref.shape[0])
    stat = jnp.zeros(stat_ref.shape, jnp.float32)
    for h, cols in enumerate(head_slices(q_ref.shape[1])):
        out, log_total = attend_head(q_ref[:, cols], k_ref[:, cols], v_ref[:, cols], scale)
        out_ref[:, cols] = out.astype(jnp.bfloat16)
        stat = jnp.where(lane == h, log_total, stat)
    stat_ref[...] = stat


def far_merge_kernel(
    index_ref, live_ref, q_ref, k_ref, v_ref, got_ref, got_stat_ref, out_ref, stat_ref, *, scale
):
    live = live_ref[0] > 0
    lane = lanes(q_ref.shape[0])
    stat = jnp.zeros(stat_ref.shape, jnp.float32)
    for h, cols in enumerate(head_slices(q_ref.shape[1])):
        out, log_total = attend_head(q_ref[:, cols], k_ref[:, cols], v_ref[:, cols], scale)
        got_log = jnp.where(live, got_stat_ref[:, h : h + 1], neg_big)
        out, log_total = merged(out, log_total, got_ref[:, cols].astype(jnp.float32), got_log)
        out_ref[:, cols] = out.astype(jnp.bfloat16)
        stat = jnp.where(lane == h, log_total, stat)
    stat_ref[...] = stat


def own_forward_kernel(
    live_ref, q_ref, g_ref, k_ref, v_ref, got_ref, got_stat_ref, out_ref, stat_ref, *, scale
):
    live = live_ref[0] > 0
    lane = lanes(q_ref.shape[0])
    stat = jnp.zeros(stat_ref.shape, jnp.float32)
    for h, cols in enumerate(head_slices(q_ref.shape[1])):
        out, log_total = attend_head(q_ref[:, cols], k_ref[:, cols], v_ref[:, cols], scale)
        got_log = jnp.where(live, got_stat_ref[:, h : h + 1], neg_big)
        out, log_total = merged(out, log_total, got_ref[:, cols].astype(jnp.float32), got_log)
        low = out.astype(jnp.bfloat16)
        out_ref[:, cols] = low
        delta = jnp.sum(
            g_ref[:, cols].astype(jnp.float32) * low.astype(jnp.float32), axis=-1, keepdims=True
        )
        stat = jnp.where(lane == h, log_total, stat)
        stat = jnp.where(lane == DELTA_LANE + h, delta, stat)
    stat_ref[...] = stat


def head_grads(q, g, k, v, log_total, delta, scale):
    probs = jnp.exp(rows_by_rows(q, k) * scale - log_total)
    dscore = (probs * (rows_by_rows(g, v) - delta)).astype(jnp.bfloat16)
    query_part = plain(dscore, k) * scale
    key_part = turned(dscore, q) * scale
    value_part = turned(probs.astype(jnp.bfloat16), g)
    return query_part, key_part, value_part


def own_backward_kernel(
    q_ref, g_ref, k_ref, v_ref, stat_ref, query_ref, key_ref, value_ref, *, scale
):
    for h, cols in enumerate(head_slices(q_ref.shape[1])):
        query_part, key_part, value_part = head_grads(
            q_ref[:, cols],
            g_ref[:, cols],
            k_ref[:, cols],
            v_ref[:, cols],
            stat_ref[:, h : h + 1],
            stat_ref[:, DELTA_LANE + h : DELTA_LANE + h + 1],
            scale,
        )
        query_ref[:, cols] = query_part
        key_ref[:, cols] = key_part.astype(jnp.bfloat16)
        value_ref[:, cols] = value_part.astype(jnp.bfloat16)


def far_backward_kernel(index_ref, *refs, scale, count):
    far = [refs[0:5], refs[5:10]]
    own_key_ref, own_value_ref = refs[10:12]
    query_refs = refs[12:14]
    key_ref, value_ref, key_sum, value_sum = refs[14:18]
    i = pl.program_id(0)

    @pl.when(i == 0)
    def _():
        key_sum[...] = own_key_ref[...].astype(jnp.float32)
        value_sum[...] = own_value_ref[...].astype(jnp.float32)

    for step in range(NSTR):
        q_ref, g_ref, k_ref, v_ref, stat_ref = far[step]
        start = pl.multiple_of(index_ref[step * count + i] * FBLK, FBLK)
        rows = pl.ds(start, FBLK)
        for h, cols in enumerate(head_slices(q_ref.shape[1])):
            query_part, key_part, value_part = head_grads(
                q_ref[:, cols],
                g_ref[:, cols],
                k_ref[:, cols],
                v_ref[:, cols],
                stat_ref[:, h : h + 1],
                stat_ref[:, DELTA_LANE + h : DELTA_LANE + h + 1],
                scale,
            )
            query_refs[step][:, cols] = query_part.astype(jnp.bfloat16)
            key_sum[rows, cols] += key_part
            value_sum[rows, cols] += value_part

    @pl.when(i == pl.num_programs(0) - 1)
    def _():
        key_ref[...] = key_sum[...].astype(jnp.bfloat16)
        value_ref[...] = value_sum[...].astype(jnp.bfloat16)


def params():
    return pltpu.CompilerParams(vmem_limit_bytes=56 * 2**20)


def cost(flops, size):
    return pl.CostEstimate(flops=flops, bytes_accessed=size, transcendentals=0)


def shape(rows, width, kind):
    return jax.ShapeDtypeStruct((rows, width), kind)


def one_context(fine, query, value_weight, list_rows, grad):
    seq_count = lax.axis_size("seq")
    me = lax.axis_index("seq")
    row_count, width = fine.shape
    scale = 1.0 / math.sqrt(width // HEADS)
    fine_count = row_count // FBLK
    query_rows = query.shape[0]
    count = query_rows // QBLK
    own_count = list_rows.shape[1] - NSTR
    own_rows = own_count * FBLK
    stride = seq_count // (NSTR + 1)
    low, full = jnp.bfloat16, jnp.float32

    def served(step):
        peer = lax.dynamic_slice_in_dim(list_rows, (me + (step + 1) * stride) * count, count, 0)
        return jnp.clip(peer[:, own_count + step] - me * fine_count, 0, fine_count - 1)

    index = [served(step) for step in range(NSTR)]
    live = (me >= stride).astype(jnp.int32).reshape(1)

    q1 = shifted(query, -stride)
    values = plain(fine, value_weight).astype(low)
    q2 = shifted(q1, -stride)
    held_grad, q2 = lax.optimization_barrier((grad, q2))
    g1 = shifted(held_grad, -stride)
    g2 = shifted(g1, -stride)

    here = pl.BlockSpec((QBLK, width), lambda i, *_: (i, 0))
    stat_here = pl.BlockSpec((QBLK, 128), lambda i, *_: (i, 0))
    listed = pl.BlockSpec((FBLK, width), lambda i, index, *_: (index[i], 0))
    own = pl.BlockSpec((own_rows, width), lambda i, *_: (i, 0))
    far_flops = 4 * query_rows * FBLK * width
    out_shapes = (shape(query_rows, width, low), shape(query_rows, 128, full))

    o2, s2 = pl.pallas_call(
        functools.partial(far_first_kernel, scale=scale),
        out_shape=out_shapes,
        grid_spec=pltpu.PrefetchScalarGridSpec(
            num_scalar_prefetch=1,
            grid=(count,),
            in_specs=[here, listed, listed],
            out_specs=(here, stat_here),
        ),
        compiler_params=params(),
        cost_estimate=cost(far_flops, 8 * query_rows * width),
        name="far_first",
    )(index[1], q2, fine, values)
    got_o2, got_s2 = shifted(o2, stride), shifted(s2, stride)
    o1, s1 = pl.pallas_call(
        functools.partial(far_merge_kernel, scale=scale),
        out_shape=out_shapes,
        grid_spec=pltpu.PrefetchScalarGridSpec(
            num_scalar_prefetch=2,
            grid=(count,),
            in_specs=[here, listed, listed, here, stat_here],
            out_specs=(here, stat_here),
        ),
        compiler_params=params(),
        cost_estimate=cost(far_flops, 10 * query_rows * width),
        name="far_merge",
    )(index[0], live, q1, fine, values, got_o2, got_s2)
    got_o1, got_s1 = shifted(o1, stride), shifted(s1, stride)
    attended, stat = pl.pallas_call(
        functools.partial(own_forward_kernel, scale=scale),
        out_shape=out_shapes,
        grid_spec=pltpu.PrefetchScalarGridSpec(
            num_scalar_prefetch=1,
            grid=(count,),
            in_specs=[here, here, own, own, here, stat_here],
            out_specs=(here, stat_here),
        ),
        compiler_params=params(),
        cost_estimate=cost(2 * far_flops, 24 * query_rows * width),
        name="own_forward",
    )(live, query, grad, fine, values, got_o1, got_s1)
    stat1 = shifted(stat, -stride)
    stat2 = shifted(stat, -2 * stride)
    own_query, own_key, own_value = pl.pallas_call(
        functools.partial(own_backward_kernel, scale=scale),
        out_shape=(
            shape(query_rows, width, full),
            shape(row_count, width, low),
            shape(row_count, width, low),
        ),
        grid=(count,),
        in_specs=[here, here, own, own, stat_here],
        out_specs=(here, own, own),
        compiler_params=params(),
        cost_estimate=cost(5 * far_flops, 40 * query_rows * width),
        name="own_backward",
    )(query, grad, fine, values, stat)

    def listed_by(step):
        return pl.BlockSpec((FBLK, width), lambda i, index: (index[step * count + i], 0))

    whole = pl.BlockSpec((row_count, width), lambda i, *_: (0, 0), pipeline_mode=pl.Buffered(1))
    far_query1, far_query2, key_sum, value_total = pl.pallas_call(
        functools.partial(far_backward_kernel, scale=scale, count=count),
        out_shape=(
            shape(query_rows, width, low),
            shape(query_rows, width, low),
            shape(row_count, width, low),
            shape(row_count, width, low),
        ),
        grid_spec=pltpu.PrefetchScalarGridSpec(
            num_scalar_prefetch=1,
            grid=(count,),
            in_specs=[here, here, listed_by(0), listed_by(0), stat_here]
            + [here, here, listed_by(1), listed_by(1), stat_here]
            + [whole, whole],
            out_specs=(here, here, whole, whole),
            scratch_shapes=[
                pltpu.VMEM((row_count, width), full),
                pltpu.VMEM((row_count, width), full),
            ],
        ),
        compiler_params=params(),
        cost_estimate=cost(5 * far_flops, 50 * query_rows * width),
        name="far_backward",
    )(
        jnp.concatenate(index),
        q1, g1, fine, values, stat1,
        q2, g2, fine, values, stat2,
        own_key, own_value,
    )
    got_query2 = shifted(far_query2, stride)
    chain = (far_query1.astype(full) + got_query2.astype(full)).astype(low)
    got_query = shifted(chain, stride)
    query_grad = (own_query + got_query.astype(full)).astype(low)
    back_rows = rows_by_rows(value_total, value_weight)
    row_grad = (key_sum.astype(full) + back_rows).astype(low)
    return attended, query_grad, row_grad, value_total


def shards(fine_rows, queries, value_weight, block_lists, out_grad):
    attended, query_grad, row_grad, value_total = one_context(
        fine_rows[0], queries[0], value_weight, block_lists[0], out_grad[0]
    )
    weight_part = turned(fine_rows[0], value_total).astype(jnp.bfloat16)
    weight_share = lax.psum_scatter(weight_part, "seq", scatter_dimension=0, tiled=True)
    weight_grad = lax.psum(weight_share.astype(jnp.float32), "dp")
    return attended[None], query_grad[None], row_grad[None], weight_grad


def solution(mesh):
    return jax.shard_map(
        shards,
        mesh=mesh,
        in_specs=(
            P("dp", "seq", None),
            P("dp", "seq", None),
            P(),
            P("dp", None, None),
            P("dp", "seq", None),
        ),
        out_specs=(
            P("dp", "seq", None),
            P("dp", "seq", None),
            P("dp", "seq", None),
            P("seq", None),
        ),
        check_vma=False,
    )
```

time: 545 us -> 365 us (0.67); the launches traced: 535 us -> 364 us
  local copies, waits for them, and re-layouts: 139 us -> 15.9 us
  Pallas kernels: 0 us -> 98.6 us
  matrix products: 108 us -> 27.9 us
  waiting for transfers between devices: 178 us -> 113 us
  blocking collectives: 0 us -> 57.7 us
  starting transfers between devices: 79.4 us -> 34.1 us
  other arithmetic: 14.2 us -> 3.36 us
    pallas_call x0 -> x5, Pallas kernels: none -> 98.6 us  [the longest x1 31.7 us: one_context(): pl.pallas_call(functools.partial(far_backward_kernel, scale=scale, count=...]
    dot_general x27 -> x3, matrix products: 108 us -> 27.9 us  [the longest x1 9.88 us: rows_by_rows(): lax.dot_general(a, b, (((1,), (1,)), ((), ())), preferred_element_type=jn...]
    ppermute x18 -> x12, waiting for transfers between devices: 24 us -> 103 us  [shifted(): return lax.ppermute(block, 'seq', route)]
    psum x1 -> x0, waiting for transfers between devices: 77.9 us -> none  [shards(): weight_grad = lax.psum(weight_share, 'dp')]
    unnamed x3 -> x2, waiting for transfers between devices: 76.6 us -> 9.17 us
    psum x0 -> x1, blocking collectives: none -> 57.7 us  [shards(): weight_grad = lax.psum(weight_share.astype(jnp.float32), 'dp')]
    ppermute x18 -> x12, starting transfers between devices: 79.3 us -> 34.1 us  [shifted(): return lax.ppermute(block, 'seq', route)]
    another operation x13 -> x0, local copies, waits for them, and re-layouts: 42 us -> none  [the longest x4 19.1 us: add_blocks(): value_rows = value_part.reshape(-1, FBLK, model_width)]
  transfers between devices with their start and end apart: 20 -> 13, of which waited for: 7 -> 7; matrix products, arithmetic and copies ran while one was open for 40% -> 6% of each run, Pallas kernels for 0% -> 14%
where the time goes in v1:
time: 365 us; the launch traced here: 364 us
  waiting for transfers between devices  113 us (31%)
  Pallas kernels  98.6 us (27%)
  blocking collectives  57.7 us (16%)
  starting transfers between devices  34.1 us (9%)
  matrix products  27.9 us (8%)
  local copies, waits for them, and re-layouts  15.9 us (4%)
  between operations  14.3 us (4%)
    ppermute x12, waiting for transfers between devices, shifted(): return lax.ppermute(block, 'seq', route)  103 us
    psum x1, blocking collectives, shards(): weight_grad = lax.psum(weight_share.astype(jnp.float32), 'dp')  57.7 us
    ppermute x12, starting transfers between devices, shifted(): return lax.ppermute(block, 'seq', route)  34.1 us
    pallas_call x1, Pallas kernels, one_context(): pl.pallas_call(functools.partial(far_backward_kernel, scale=scale, count=...  31.7 us
    pallas_call x1, Pallas kernels, one_context(): pl.pallas_call(functools.partial(own_forward_kernel, scale=scale), out_sh...  19.7 us
    pallas_call x1, Pallas kernels, one_context(): pl.pallas_call(functools.partial(far_merge_kernel, scale=scale), out_shap...  17.4 us
    pallas_call x1, Pallas kernels, one_context(): pl.pallas_call(functools.partial(own_backward_kernel, scale=scale), out_s...  15.3 us
    unnamed x37, local copies, waits for them, and re-layouts  14.9 us
  transfers between devices with their start and end apart: 13, of which 7 were waited for; matrix products, arithmetic and copies ran while one was open for 6% of the time, Pallas kernels for 14%

profile of v1, /device:TPU:0, one launch (start us, length us, event | category | flops | bytes accessed | tf_op | source)
XLA Modules:
  0.0 364.4 jit_solution(7434989908477131474)
XLA Ops:
  10.2 19.7 %collective-permute-done.q_ref.refs_0_ = bf16[256,1536]{1,0:T(8,128)(2,1)S(1)} collective-permute-done((bf16[256,1536]{1,0:T(8,128)(2,1)}, bf16[256,1536]{1,0:T(8,128)(2,1)S(1)}, u32[]{:S(2)}, u32[]{:S(2)}) %collective-permute-start) | collective-permute-done | bytes 786464 | tf_op jit(solution)/shard_map/ppermute | solution.py:23
  31.2 9.2 %convolution_convert_fusion.1.v_ref.refs_3_.refs_8_ = bf16[1024,1536]{1,0:T(8,128)(2,1)} fusion(bf16[1536,1536]{1,0:T(8,128)(2,1)} %param.7, bf16[1,1024,1536]{2,1,0:T(8,128)(2,1)} %param.5), kind=kOutput, calls=%fused_computation.3 | convolution fusion | flops 4833411072 | bytes 11010048 | tf_op jit(solution)/shard_map/dot_general | solution.py:35
  40.4 10.1 %collective-permute-done.1.q_ref.refs_5_ = bf16[256,1536]{1,0:T(8,128)(2,1)S(1)} collective-permute-done((bf16[256,1536]{1,0:T(8,128)(2,1)S(1)}, bf16[256,1536]{1,0:T(8,128)(2,1)S(1)}, u32[]{:S(2)}, u32[]{:S(2)}) %collective-permute-start.1) | collective-permute-done | bytes 786464 | tf_op jit(solution)/shard_map/ppermute | solution.py:23
  51.4 14.6 %far_first.1 = (bf16[256,1536]{1,0:T(8,128)(2,1)}, f32[256,128]{1,0:T(8,128)}) custom-call(s32[4]{0:T(128)} %clamp_reduce_fusion.index_ref, bf16[256,1536]{1,0:T(8,128)(2,1)} %copy-done.2, bf16[1024,1536]{1,0:T(8,128)(2,1)} %bitcast.22, bf16[1024,1536]{1,0:T(8,128)(2,1)} %convolution_convert_fusion.1.v_ref.refs_3_.refs_8_), custom_call_target="tpu_custom_call" | custom-call | flops 201326592 | bytes 3145728 | tf_op jit(solution)/shard_map/far_first/pallas_call | solution.py:218
  66.0 3.4 collective-permute-start.2
  70.7 4.6 %collective-permute-start.3 = (f32[256,128]{1,0:T(8,128)}, f32[256,128]{1,0:T(8,128)S(1)}, u32[]{:S(2)}, u32[]{:S(2)}) collective-permute-start(f32[256,128]{1,0:T(8,128)} %get-tuple-element.21), channel_id=1, source_target_pairs={{0,2},{1,3},{2,4},{3,5},{4,6},{5,7},{8,10},{9,11},{10,12},{11,13},... | collective-permute-start | bytes 393224 | tf_op jit(solution)/shard_map/ppermute | solution.py:23
  76.1 11.3 %collective-permute-done.3.got_stat_ref = f32[256,128]{1,0:T(8,128)S(1)} collective-permute-done((f32[256,128]{1,0:T(8,128)}, f32[256,128]{1,0:T(8,128)S(1)}, u32[]{:S(2)}, u32[]{:S(2)}) %collective-permute-start.3) | collective-permute-done | bytes 131104 | tf_op jit(solution)/shard_map/ppermute | solution.py:23
  88.4 17.4 %far_merge.1 = (bf16[256,1536]{1,0:T(8,128)(2,1)}, f32[256,128]{1,0:T(8,128)}) custom-call(s32[4]{0:T(128)} %clamp_reduce_fusion.1.index_ref, s32[1]{0:T(128)} %bitcast.live_ref, bf16[256,1536]{1,0:T(8,128)(2,1)} %copy-done.1, bf16[1024,1536]{1,0:T(8,128)(2,1)} %bitcast.23, bf16[1024,1536]{1,0:T(8,128)(2,1)} %convolution_convert_fusion.1.v_ref.refs_3_.refs_8_, ...), custom_call_target="tpu_custom_call" | custom-call | flops 201326592 | bytes 3932160 | tf_op jit(solution)/shard_map/far_merge/pallas_call | solution.py:232
  105.7 4.3 %collective-permute-start.4 = (bf16[256,1536]{1,0:T(8,128)(2,1)}, bf16[256,1536]{1,0:T(8,128)(2,1)S(1)}, u32[]{:S(2)}, u32[]{:S(2)}) collective-permute-start(bf16[256,1536]{1,0:T(8,128)(2,1)} %get-tuple-element.22), channel_id=1, source_target_pairs={{0,2},{1,3},{2,4},{3,5},{4,6},{5,7},{8,10},{9,11},{10,12},{11,13},... | collective-permute-start | bytes 2359304 | tf_op jit(solution)/shard_map/ppermute | solution.py:23
  111.4 4.6 %collective-permute-start.5 = (f32[256,128]{1,0:T(8,128)}, f32[256,128]{1,0:T(8,128)S(1)}, u32[]{:S(2)}, u32[]{:S(2)}) collective-permute-start(f32[256,128]{1,0:T(8,128)} %get-tuple-element.23), channel_id=1, source_target_pairs={{0,2},{1,3},{2,4},{3,5},{4,6},{5,7},{8,10},{9,11},{10,12},{11,13},... | collective-permute-start | bytes 393224 | tf_op jit(solution)/shard_map/ppermute | solution.py:23
  115.9 11.2 %collective-permute-done.5.got_stat_ref = f32[256,128]{1,0:T(8,128)S(1)} collective-permute-done((f32[256,128]{1,0:T(8,128)}, f32[256,128]{1,0:T(8,128)S(1)}, u32[]{:S(2)}, u32[]{:S(2)}) %collective-permute-start.5) | collective-permute-done | bytes 131104 | tf_op jit(solution)/shard_map/ppermute | solution.py:23
  128.7 19.7 %own_forward.1 = (bf16[256,1536]{1,0:T(8,128)(2,1)}, f32[256,128]{1,0:T(8,128)}) custom-call(s32[1]{0:T(128)} %bitcast.live_ref, bf16[256,1536]{1,0:T(8,128)(2,1)} %bitcast.29, bf16[256,1536]{1,0:T(8,128)(2,1)} %bitcast.31, bf16[1024,1536]{1,0:T(8,128)(2,1)} %bitcast.24, bf16[1024,1536]{1,0:T(8,128)(2,1)} %convolution_convert_fusion.1.v_ref.refs_3_.refs_8_, ...), custom_call_target="tpu_custom_call" | custom-call | flops 402653184 | bytes 9437184 | tf_op jit(solution)/shard_map/own_forward/pallas_call | solution.py:246
  149.7 1.5 collective-permute-start.7
  151.8 15.3 %own_backward.1 = (f32[256,1536]{1,0:T(8,128)}, bf16[1024,1536]{1,0:T(8,128)(2,1)}, bf16[1024,1536]{1,0:T(8,128)(2,1)}) custom-call(bf16[256,1536]{1,0:T(8,128)(2,1)} %bitcast.30, bf16[256,1536]{1,0:T(8,128)(2,1)} %bitcast.32, bf16[1024,1536]{1,0:T(8,128)(2,1)} %bitcast.25, bf16[1024,1536]{1,0:T(8,128)(2,1)} %convolution_convert_fusion.1.v_ref.refs_3_.refs_8_, ...), custom_call_target="tpu_custom_call" | custom-call | flops 1006632960 | bytes 15728640 | tf_op jit(solution)/shard_map/own_backward/pallas_call | solution.py:261
  168.1 31.7 %far_backward.1 = (bf16[256,1536]{1,0:T(8,128)(2,1)}, bf16[256,1536]{1,0:T(8,128)(2,1)}, bf16[1024,1536]{1,0:T(8,128)(2,1)}, bf16[1024,1536]{1,0:T(8,128)(2,1)}) custom-call(s32[8]{0:T(128)} %pad_add_fusion.index_ref, bf16[256,1536]{1,0:T(8,128)(2,1)} %copy-done.1, bf16[256,1536]{1,0:T(8,128)(2,1)} %copy-done.5, bf16[1024,1536]{1,0:T(8,128)(2,1)} %bitcast.26, ...), custom_call_target="tpu_custom_call" | custom-call | flops 1006632960 | bytes 19660800 | tf_op jit(solution)/shard_map/far_backward/pallas_call | solution.py:280
  199.8 8.8 %fusion = bf16[1536,1536]{0,1:T(8,128)(2,1)} fusion(bf16[1024,1536]{1,0:T(8,128)(2,1)} %get-tuple-element.33, bf16[1,1024,1536]{2,1,0:T(8,128)(2,1)S(1)} %copy-done), kind=kOutput, calls=%fused_computation.1 | convolution fusion | flops 4834197504 | bytes 11010048 | tf_op jit(solution)/shard_map/dot_general | solution.py:31
  208.6 6.6 %copy.18 = bf16[1536,1536]{1,0:T(8,128)(2,1)} copy(bf16[1536,1536]{0,1:T(8,128)(2,1)} %fusion) | data formatting | bytes 9437184
  216.4 4.9 %collective-permute-start.10 = (bf16[256,1536]{1,0:T(8,128)(2,1)S(1)}, bf16[256,1536]{1,0:T(8,128)(2,1)S(1)}, u32[]{:S(2)}, u32[]{:S(2)}) collective-permute-start(bf16[256,1536]{1,0:T(8,128)(2,1)S(1)} %copy-done.16), channel_id=1, source_target_pairs={{0,2},{1,3},{2,4},{3,5},{4,6},{5,7},{8,10},{9,11},{10,12},{11,13},... | collective-permute-start | bytes 2359304 | tf_op jit(solution)/shard_map/ppermute | solution.py:23
  221.3 31.0 %collective-permute-done.10 = bf16[256,1536]{1,0:T(8,128)(2,1)S(1)} collective-permute-done((bf16[256,1536]{1,0:T(8,128)(2,1)S(1)}, bf16[256,1536]{1,0:T(8,128)(2,1)S(1)}, u32[]{:S(2)}, u32[]{:S(2)}) %collective-permute-start.10) | collective-permute-done | bytes 786464 | tf_op jit(solution)/shard_map/ppermute | solution.py:23
  252.5 4.4 %collective-permute-start.11 = (bf16[256,1536]{1,0:T(8,128)(2,1)S(1)}, bf16[256,1536]{1,0:T(8,128)(2,1)S(1)}, u32[]{:S(2)}, u32[]{:S(2)}) collective-permute-start(bf16[256,1536]{1,0:T(8,128)(2,1)S(1)} %add_convert_fusion.2), channel_id=1, source_target_pairs={{0,2},{1,3},{2,4},{3,5},{4,6},{5,7},{8,10},{9,11},{10,12},{11,13},... | collective-permute-start | bytes 2359304 | tf_op jit(solution)/shard_map/ppermute | solution.py:23
  257.0 9.9 %fusion.1 = bf16[1,1024,1536]{2,1,0:T(8,128)(2,1)} fusion(bf16[1024,1536]{1,0:T(8,128)(2,1)} %get-tuple-element.32, bf16[1024,1536]{1,0:T(8,128)(2,1)} %get-tuple-element.33, bf16[1536,1536]{1,0:T(8,128)(2,1)} %param.7), kind=kOutput, calls=%fused_computation.4 | convolution fusion | flops 4836556800 | bytes 14155776 | tf_op jit(solution)/shard_map/dot_general | solution.py:27
  266.8 19.9 %collective-permute-done.11 = bf16[256,1536]{1,0:T(8,128)(2,1)S(1)} collective-permute-done((bf16[256,1536]{1,0:T(8,128)(2,1)S(1)}, bf16[256,1536]{1,0:T(8,128)(2,1)S(1)}, u32[]{:S(2)}, u32[]{:S(2)}) %collective-permute-start.11) | collective-permute-done | bytes 786464 | tf_op jit(solution)/shard_map/ppermute | solution.py:23
  287.8 9.2 %reduce-scatter.4.cloned.1.call-done = bf16[192,1536]{1,0:T(8,128)(2,1)} async-done(((bf16[1536,1536]{1,0:T(8,128)(2,1)}), bf16[192,1536]{1,0:T(8,128)(2,1)}) %reduce-scatter.4.cloned.1.call-update) | async-done | bytes 589840
  298.3 57.7 %all-reduce.1 = f32[192,1536]{0,1:T(8,128)S(1)} all-reduce(bf16[192,1536]{0,1:T(8,128)(2,1)S(1)} %copy.19), channel_id=1, replica_groups=mesh['dp'=4,'seq'=8] {'dp'}, use_global_device_ids=true, to_apply=%region_1.2 | all-reduce | flops 294912 | bytes 1769472 | tf_op jit(solution)/shard_map/psum | solution.py:324
  (57 shorter events, 19.1 us)
Async XLA Ops:
  7.2 289.8 %reduce-scatter.4.cloned.1.call-start = ((), (), s32[]{:S(2)}) async-start(), calls=%async_computation.1 | async-start | bytes 5308416
  7.2 22.7 %collective-permute-start = (bf16[256,1536]{1,0:T(8,128)(2,1)}, bf16[256,1536]{1,0:T(8,128)(2,1)S(1)}, u32[]{:S(2)}, u32[]{:S(2)}) collective-permute-start(bf16[256,1536]{1,0:T(8,128)(2,1)} %bitcast.28), channel_id=1, source_target_pairs={{2,0},{3,1},{4,2},{5,3},{6,4},{7,5},{10,8},{11,9},{12,10},{13,11},... | collective-permute-start | bytes 2359304 | tf_op jit(solution)/shard_map/ppermute | solution.py:23
  29.9 10.5 %copy-start.1 = (bf16[256,1536]{1,0:T(8,128)(2,1)}, bf16[256,1536]{1,0:T(8,128)(2,1)S(1)}, u32[]{:S(2)}) copy-start(bf16[256,1536]{1,0:T(8,128)(2,1)S(1)} %collective-permute-done.q_ref.refs_0_) | copy-start | bytes 2359300
  29.9 20.6 %collective-permute-start.1 = (bf16[256,1536]{1,0:T(8,128)(2,1)S(1)}, bf16[256,1536]{1,0:T(8,128)(2,1)S(1)}, u32[]{:S(2)}, u32[]{:S(2)}) collective-permute-start(bf16[256,1536]{1,0:T(8,128)(2,1)S(1)} %collective-permute-done.q_ref.refs_0_), channel_id=1, source_target_pairs={{2,0},{3,1},{4,2},{5,3},{6,4},{7,5},{10,8},{11,9},{12,10},{13,11},... | collective-permute-start | bytes 2359304 | tf_op jit(solution)/shard_map/ppermute | solution.py:23
  51.4 18.0 %copy-start.3 = (bf16[1,256,1536]{2,1,0:T(8,128)(2,1)S(1)}, bf16[1,256,1536]{2,1,0:T(8,128)(2,1)}, u32[]{:S(2)}) copy-start(bf16[1,256,1536]{2,1,0:T(8,128)(2,1)} %param.9) | copy-start | bytes 2359300
  66.0 21.4 %collective-permute-start.2 = (bf16[256,1536]{1,0:T(8,128)(2,1)}, bf16[256,1536]{1,0:T(8,128)(2,1)S(1)}, u32[]{:S(2)}, u32[]{:S(2)}) collective-permute-start(bf16[256,1536]{1,0:T(8,128)(2,1)} %get-tuple-element.20), channel_id=1, source_target_pairs={{0,2},{1,3},{2,4},{3,5},{4,6},{5,7},{8,10},{9,11},{10,12},{11,13},... | collective-permute-start | bytes 2359304 | tf_op jit(solution)/shard_map/ppermute | solution.py:23
  69.4 40.7 %collective-permute-start.6 = (bf16[256,1536]{1,0:T(8,128)(2,1)S(1)}, bf16[256,1536]{1,0:T(8,128)(2,1)S(1)}, u32[]{:S(2)}, u32[]{:S(2)}) collective-permute-start(bf16[256,1536]{1,0:T(8,128)(2,1)S(1)} %bitcast.33), channel_id=1, source_target_pairs={{2,0},{3,1},{4,2},{5,3},{6,4},{7,5},{10,8},{11,9},{12,10},{13,11},... | collective-permute-start | bytes 2359304 | tf_op jit(solution)/shard_map/ppermute | solution.py:23
  70.7 16.8 %collective-permute-start.3 = (f32[256,128]{1,0:T(8,128)}, f32[256,128]{1,0:T(8,128)S(1)}, u32[]{:S(2)}, u32[]{:S(2)}) collective-permute-start(f32[256,128]{1,0:T(8,128)} %get-tuple-element.21), channel_id=1, source_target_pairs={{0,2},{1,3},{2,4},{3,5},{4,6},{5,7},{8,10},{9,11},{10,12},{11,13},... | collective-permute-start | bytes 393224 | tf_op jit(solution)/shard_map/ppermute | solution.py:23
  105.7 21.5 %collective-permute-start.4 = (bf16[256,1536]{1,0:T(8,128)(2,1)}, bf16[256,1536]{1,0:T(8,128)(2,1)S(1)}, u32[]{:S(2)}, u32[]{:S(2)}) collective-permute-start(bf16[256,1536]{1,0:T(8,128)(2,1)} %get-tuple-element.22), channel_id=1, source_target_pairs={{0,2},{1,3},{2,4},{3,5},{4,6},{5,7},{8,10},{9,11},{10,12},{11,13},... | collective-permute-start | bytes 2359304 | tf_op jit(solution)/shard_map/ppermute | solution.py:23
  110.0 38.3 %copy-start.5 = (bf16[256,1536]{1,0:T(8,128)(2,1)}, bf16[256,1536]{1,0:T(8,128)(2,1)S(1)}, u32[]{:S(2)}) copy-start(bf16[256,1536]{1,0:T(8,128)(2,1)S(1)} %collective-permute-done.6.refs_1_) | copy-start | bytes 2359300
  110.1 57.0 %collective-permute-start.8 = (bf16[256,1536]{1,0:T(8,128)(2,1)S(1)}, bf16[256,1536]{1,0:T(8,128)(2,1)S(1)}, u32[]{:S(2)}, u32[]{:S(2)}) collective-permute-start(bf16[256,1536]{1,0:T(8,128)(2,1)S(1)} %collective-permute-done.6.refs_1_), channel_id=1, source_target_pairs={{2,0},{3,1},{4,2},{5,3},{6,4},{7,5},{10,8},{11,9},{12,10},{13,11},... | collective-permute-start | bytes 2359304 | tf_op jit(solution)/shard_map/ppermute | solution.py:23
  111.4 39.8 %copy-start.14 = (s32[4]{0:T(128)S(1)}, s32[4]{0:T(128)}, u32[]{:S(2)}) copy-start(s32[4]{0:T(128)} %clamp_reduce_fusion.index_ref) | copy-start | bytes 52
  111.4 39.8 %copy-start.15 = (s32[4]{0:T(128)S(1)}, s32[4]{0:T(128)}, u32[]{:S(2)}) copy-start(s32[4]{0:T(128)} %clamp_reduce_fusion.1.index_ref) | copy-start | bytes 52
  111.4 15.8 %collective-permute-start.5 = (f32[256,128]{1,0:T(8,128)}, f32[256,128]{1,0:T(8,128)S(1)}, u32[]{:S(2)}, u32[]{:S(2)}) collective-permute-start(f32[256,128]{1,0:T(8,128)} %get-tuple-element.23), channel_id=1, source_target_pairs={{0,2},{1,3},{2,4},{3,5},{4,6},{5,7},{8,10},{9,11},{10,12},{11,13},... | collective-permute-start | bytes 393224 | tf_op jit(solution)/shard_map/ppermute | solution.py:23
  148.4 18.7 %collective-permute-start.9 = (f32[256,128]{1,0:T(8,128)}, f32[256,128]{1,0:T(8,128)S(1)}, u32[]{:S(2)}, u32[]{:S(2)}) collective-permute-start(f32[256,128]{1,0:T(8,128)} %get-tuple-element.25.stat_ref), channel_id=1, source_target_pairs={{4,0},{5,1},{6,2},{7,3},{12,8},{13,9},{14,10},{15,11},{20,16},{21,... | collective-permute-start | bytes 393224 | tf_op jit(solution)/shard_map/ppermute | solution.py:23
  149.7 17.4 %collective-permute-start.7 = (f32[256,128]{1,0:T(8,128)}, f32[256,128]{1,0:T(8,128)S(1)}, u32[]{:S(2)}, u32[]{:S(2)}) collective-permute-start(f32[256,128]{1,0:T(8,128)} %get-tuple-element.25.stat_ref), channel_id=1, source_target_pairs={{2,0},{3,1},{4,2},{5,3},{6,4},{7,5},{10,8},{11,9},{12,10},{13,11},... | collective-permute-start | bytes 393224 | tf_op jit(solution)/shard_map/ppermute | solution.py:23
  167.1 0.9 copy-start.10
  167.1 1.0 copy-start.11
  168.1 31.7 %copy-start = (bf16[1,1024,1536]{2,1,0:T(8,128)(2,1)S(1)}, bf16[1,1024,1536]{2,1,0:T(8,128)(2,1)}, u32[]{:S(2)}) copy-start(bf16[1,1024,1536]{2,1,0:T(8,128)(2,1)} %param.5) | copy-start | bytes 9437188
  215.2 1.1 copy-start.16
  215.2 37.1 %copy-start.9 = (bf16[256,1536]{1,0:T(8,128)(2,1)S(1)}, bf16[256,1536]{1,0:T(8,128)(2,1)}, u32[]{:S(2)}) copy-start(bf16[256,1536]{1,0:T(8,128)(2,1)} %get-tuple-element.30) | copy-start | bytes 2359300
  216.4 35.9 %collective-permute-start.10 = (bf16[256,1536]{1,0:T(8,128)(2,1)S(1)}, bf16[256,1536]{1,0:T(8,128)(2,1)S(1)}, u32[]{:S(2)}, u32[]{:S(2)}) collective-permute-start(bf16[256,1536]{1,0:T(8,128)(2,1)S(1)} %copy-done.16), channel_id=1, source_target_pairs={{0,2},{1,3},{2,4},{3,5},{4,6},{5,7},{8,10},{9,11},{10,12},{11,13},... | collective-permute-start | bytes 2359304 | tf_op jit(solution)/shard_map/ppermute | solution.py:23
  252.5 34.3 %collective-permute-start.11 = (bf16[256,1536]{1,0:T(8,128)(2,1)S(1)}, bf16[256,1536]{1,0:T(8,128)(2,1)S(1)}, u32[]{:S(2)}, u32[]{:S(2)}) collective-permute-start(bf16[256,1536]{1,0:T(8,128)(2,1)S(1)} %add_convert_fusion.2), channel_id=1, source_target_pairs={{0,2},{1,3},{2,4},{3,5},{4,6},{5,7},{8,10},{9,11},{10,12},{11,13},... | collective-permute-start | bytes 2359304 | tf_op jit(solution)/shard_map/ppermute | solution.py:23
  256.9 29.8 %copy-start.4 = (f32[256,1536]{1,0:T(8,128)S(1)}, f32[256,1536]{1,0:T(8,128)}, u32[]{:S(2)}) copy-start(f32[256,1536]{1,0:T(8,128)} %get-tuple-element.26) | copy-start | bytes 4718596
  (6 other events, 4.9 us)
Sparse Core Ops, SparseCore 0:
  215.4 81.5 reduce-scatter.3

commit v2 on v1

--- a/solution.py
+++ b/solution.py
@@ -40,97 +40,108 @@
     return [slice(h * size, (h + 1) * size) for h in range(HEADS)]
 
 
-def attend_head(q, k, v, scale):
-    scores = rows_by_rows(q, k) * scale
+def stacked(parts):
+    return jnp.concatenate(parts, axis=0)
+
+
+def column_of(stat_ref, first):
+    return stacked([stat_ref[:, first + h : first + h + 1] for h in range(HEADS)])
+
+
+def pieces(stack, rows):
+    return [stack[h * rows : (h + 1) * rows] for h in range(HEADS)]
+
+
+def all_scores(a_ref, b_ref):
+    return stacked([rows_by_rows(a_ref[:, c], b_ref[:, c]) for c in head_slices(a_ref.shape[1])])
+
+
+def attend(q_ref, k_ref, v_ref, scale):
+    rows, width = q_ref.shape
+    scores = all_scores(q_ref, k_ref) * scale
     top = jnp.max(scores, axis=-1, keepdims=True)
     raised = jnp.exp(scores - top)
     total = jnp.sum(raised, axis=-1, keepdims=True)
-    out = plain(raised.astype(jnp.bfloat16), v) / total
-    return out, top + jnp.log(total)
-
-
-def merged(out_a, log_a, out_b, log_b):
-    top = jnp.maximum(log_a, log_b)
-    a = jnp.exp(log_a - top)
-    b = jnp.exp(log_b - top)
-    total = a + b
-    return (out_a * a + out_b * b) / total, top + jnp.log(total)
-
-
-def lanes(rows):
-    return lax.broadcasted_iota(jnp.int32, (rows, 128), 1)
+    low = pieces(raised.astype(jnp.bfloat16), rows)
+    out = stacked([plain(low[h], v_ref[:, c]) for h, c in enumerate(head_slices(width))])
+    return out, top, total
+
+
+def write_stat(stat_ref, log_total, delta=None):
+    rows = stat_ref.shape[0]
+    lane = lax.broadcasted_iota(jnp.int32, stat_ref.shape, 1)
+    stat = jnp.zeros(stat_ref.shape, jnp.float32)
+    for h, part in enumerate(pieces(log_total, rows)):
+        stat = jnp.where(lane == h, part, stat)
+    if delta is not None:
+        for h, part in enumerate(pieces(delta, rows)):
+            stat = jnp.where(lane == DELTA_LANE + h, part, stat)
+    stat_ref[...] = stat
+
+
+def write_out(out_ref, out):
+    rows, width = out_ref.shape
+    for part, cols in zip(pieces(out, rows), head_slices(width)):
+        out_ref[:, cols] = part.astype(out_ref.dtype)
+
+
+def stack_of(ref):
+    return stacked([ref[:, c] for c in head_slices(ref.shape[1])])
 
 
 def far_first_kernel(index_ref, q_ref, k_ref, v_ref, out_ref, stat_ref, *, scale):
-    lane = lanes(q_ref.shape[0])
-    stat = jnp.zeros(stat_ref.shape, jnp.float32)
-    for h, cols in enumerate(head_slices(q_ref.shape[1])):
-        out, log_total = attend_head(q_ref[:, cols], k_ref[:, cols], v_ref[:, cols], scale)
-        out_ref[:, cols] = out.astype(jnp.bfloat16)
-        stat = jnp.where(lane == h, log_total, stat)
-    stat_ref[...] = stat
+    out, top, total = attend(q_ref, k_ref, v_ref, scale)
+    write_out(out_ref, out * (1.0 / total))
+    write_stat(stat_ref, top + jnp.log(total))
+
+
+def attend_and_merge(live_ref, q_ref, k_ref, v_ref, got_ref, got_stat_ref, scale):
+    out, top, total = attend(q_ref, k_ref, v_ref, scale)
+    got_log = jnp.where(live_ref[0] > 0, column_of(got_stat_ref, 0), neg_big)
+    most = jnp.maximum(top, got_log)
+    mine = jnp.exp(top - most)
+    other = jnp.exp(got_log - most)
+    total = total * mine + other
+    inverse = 1.0 / total
+    out = out * (mine * inverse) + stack_of(got_ref).astype(jnp.float32) * (other * inverse)
+    return out, most + jnp.log(total)
 
 
 def far_merge_kernel(
     index_ref, live_ref, q_ref, k_ref, v_ref, got_ref, got_stat_ref, out_ref, stat_ref, *, scale
 ):
-    live = live_ref[0] > 0
-    lane = lanes(q_ref.shape[0])
-    stat = jnp.zeros(stat_ref.shape, jnp.float32)
-    for h, cols in enumerate(head_slices(q_ref.shape[1])):
-        out, log_total = attend_head(q_ref[:, cols], k_ref[:, cols], v_ref[:, cols], scale)
-        got_log = jnp.where(live, got_stat_ref[:, h : h + 1], neg_big)
-        out, log_total = merged(out, log_total, got_ref[:, cols].astype(jnp.float32), got_log)
-        out_ref[:, cols] = out.astype(jnp.bfloat16)
-        stat = jnp.where(lane == h, log_total, stat)
-    stat_ref[...] = stat
+    out, log_total = attend_and_merge(live_ref, q_ref, k_ref, v_ref, got_ref, got_stat_ref, scale)
+    write_out(out_ref, out)
+    write_stat(stat_ref, log_total)
 
 
 def own_forward_kernel(
     live_ref, q_ref, g_ref, k_ref, v_ref, got_ref, got_stat_ref, out_ref, stat_ref, *, scale
 ):
-    live = live_ref[0] > 0
-    lane = lanes(q_ref.shape[0])
-    stat = jnp.zeros(stat_ref.shape, jnp.float32)
-    for h, cols in enumerate(head_slices(q_ref.shape[1])):
-        out, log_total = attend_head(q_ref[:, cols], k_ref[:, cols], v_ref[:, cols], scale)
-        got_log = jnp.where(live, got_stat_ref[:, h : h + 1], neg_big)
-        out, log_total = merged(out, log_total, got_ref[:, cols].astype(jnp.float32), got_log)
-        low = out.astype(jnp.bfloat16)
-        out_ref[:, cols] = low
-        delta = jnp.sum(
-            g_ref[:, cols].astype(jnp.float32) * low.astype(jnp.float32), axis=-1, keepdims=True
-        )
-        stat = jnp.where(lane == h, log_total, stat)
-        stat = jnp.where(lane == DELTA_LANE + h, delta, stat)
-    stat_ref[...] = stat
-
-
-def head_grads(q, g, k, v, log_total, delta, scale):
-    probs = jnp.exp(rows_by_rows(q, k) * scale - log_total)
-    dscore = (probs * (rows_by_rows(g, v) - delta)).astype(jnp.bfloat16)
-    query_part = plain(dscore, k) * scale
-    key_part = turned(dscore, q) * scale
-    value_part = turned(probs.astype(jnp.bfloat16), g)
-    return query_part, key_part, value_part
+    out, log_total = attend_and_merge(live_ref, q_ref, k_ref, v_ref, got_ref, got_stat_ref, scale)
+    low = out.astype(jnp.bfloat16)
+    write_out(out_ref, low)
+    delta = jnp.sum(
+        stack_of(g_ref).astype(jnp.float32) * low.astype(jnp.float32), axis=-1, keepdims=True
+    )
+    write_stat(stat_ref, log_total, delta)
+
+
+def weights_of(q_ref, g_ref, k_ref, v_ref, stat_ref, scale):
+    rows = q_ref.shape[0]
+    probs = jnp.exp(all_scores(q_ref, k_ref) * scale - column_of(stat_ref, 0))
+    dscore = probs * (all_scores(g_ref, v_ref) - column_of(stat_ref, DELTA_LANE))
+    return pieces(probs.astype(jnp.bfloat16), rows), pieces(dscore.astype(jnp.bfloat16), rows)
 
 
 def own_backward_kernel(
     q_ref, g_ref, k_ref, v_ref, stat_ref, query_ref, key_ref, value_ref, *, scale
 ):
+    probs, dscore = weights_of(q_ref, g_ref, k_ref, v_ref, stat_ref, scale)
     for h, cols in enumerate(head_slices(q_ref.shape[1])):
-        query_part, key_part, value_part = head_grads(
-            q_ref[:, cols],
-            g_ref[:, cols],
-            k_ref[:, cols],
-            v_ref[:, cols],
-            stat_ref[:, h : h + 1],
-            stat_ref[:, DELTA_LANE + h : DELTA_LANE + h + 1],
-            scale,
-        )
-        query_ref[:, cols] = query_part
-        key_ref[:, cols] = key_part.astype(jnp.bfloat16)
-        value_ref[:, cols] = value_part.astype(jnp.bfloat16)
+        query_ref[:, cols] = plain(dscore[h], k_ref[:, cols]) * scale
+        key_ref[:, cols] = (turned(dscore[h], q_ref[:, cols]) * scale).astype(jnp.bfloat16)
+        value_ref[:, cols] = turned(probs[h], g_ref[:, cols]).astype(jnp.bfloat16)
 
 
 def far_backward_kernel(index_ref, *refs, scale, count):
@@ -149,24 +160,174 @@
         q_ref, g_ref, k_ref, v_ref, stat_ref = far[step]
         start = pl.multiple_of(index_ref[step * count + i] * FBLK, FBLK)
         rows = pl.ds(start, FBLK)
+        probs, dscore = weights_of(q_ref, g_ref, k_ref, v_ref, stat_ref, scale)
         for h, cols in enumerate(head_slices(q_ref.shape[1])):
-            query_part, key_part, value_part = head_grads(
-                q_ref[:, cols],
-                g_ref[:, cols],
-                k_ref[:, cols],
-                v_ref[:, cols],
-                stat_ref[:, h : h + 1],
-                stat_ref[:, DELTA_LANE + h : DELTA_LANE + h + 1],
-                scale,
+            query_refs[step][:, cols] = (plain(dscore[h], k_ref[:, cols]) * scale).astype(
+                jnp.bfloat16
             )
-            query_refs[step][:, cols] = query_part.astype(jnp.bfloat16)
-            key_sum[rows, cols] += key_part
-            value_sum[rows, cols] += value_part
+            key_sum[rows, cols] += turned(dscore[h], q_ref[:, cols]) * scale
+            value_sum[rows, cols] += turned(probs[h], g_ref[:, cols])
 
     @pl.when(i == pl.num_programs(0) - 1)
     def _():
         key_ref[...] = key_sum[...].astype(jnp.bfloat16)
         value_ref[...] = value_sum[...].astype(jnp.bfloat16)
+
+
+PIECES = 3
+
+
+def bits_of(count):
+    return count.bit_length() - 1
+
+
+def bit(index, k):
+    return lax.rem(index // (1 << k), 2)
+
+
+def plan(p, seq_count, dp_count):
+    dp_bits = list(range(bits_of(dp_count)))
+    if p % 2:
+        dp_bits = dp_bits[::-1]
+    seq_bits = list(range(1, bits_of(seq_count)))[::-1]
+    return [("seq", 0)] + [("dp", k) for k in dp_bits] + [("seq", k) for k in seq_bits]
+
+
+def stage_shapes(seq_count, dp_count, rows, width):
+    shapes = [(seq_count // 2, rows, width)]
+    for axis, _ in plan(0, seq_count, dp_count)[1:]:
+        blocks, _, cols = shapes[-1]
+        shapes.append((blocks, rows, cols // 2) if axis == "dp" else (blocks // 2, rows, cols))
+    return shapes
+
+
+def sum_kernel(seq_count, dp_count, part_ref, out_ref, *refs):
+    stages = 1 + bits_of(dp_count) + bits_of(seq_count) - 1
+    got, kept = refs[:stages], refs[stages : 2 * stages - 1]
+    gathered, send_sem, recv_sem, gather_send, gather_recv = refs[2 * stages - 1 :]
+    rows, width = part_ref.shape[3], part_ref.shape[4]
+    cols = width // dp_count
+    me = {"seq": lax.axis_index("seq"), "dp": lax.axis_index("dp")}
+
+    def partner(axis, k):
+        return {axis: me[axis] + (1 - 2 * bit(me[axis], k)) * (1 << k)}
+
+    def dp_peer(d):
+        return {"dp": lax.rem(me["dp"] + d, dp_count)}
+
+    barrier = pltpu.get_barrier_semaphore()
+    met = [("seq", k) for k in range(bits_of(seq_count))]
+    for axis, k in met:
+        pl.semaphore_signal(
+            barrier, inc=1, device_id=partner(axis, k), device_id_type=pl.DeviceIdType.MESH
+        )
+    for d in range(1, dp_count):
+        pl.semaphore_signal(
+            barrier, inc=1, device_id=dp_peer(d), device_id_type=pl.DeviceIdType.MESH
+        )
+    pl.semaphore_wait(barrier, len(met) + dp_count - 1)
+
+    def half(ref, p, s, which):
+        axis, k = plan(p, seq_count, dp_count)[s]
+        if s == 0:
+            return ref.at[:, which, p]
+        blocks, _, wide = ref.shape[1:]
+        if axis == "dp":
+            start = pl.multiple_of(which * (wide // 2), wide // 2)
+            return ref.at[p, :, :, pl.ds(start, wide // 2)]
+        return ref.at[p, pl.ds(which * (blocks // 2), blocks // 2)]
+
+    def source(s):
+        return part_ref if s == 0 else kept[s - 1]
+
+    def exchange(p, s):
+        axis, k = plan(p, seq_count, dp_count)[s]
+        return pltpu.make_async_remote_copy(
+            src_ref=half(source(s), p, s, 1 - bit(me[axis], k)),
+            dst_ref=got[s].at[p],
+            send_sem=send_sem.at[p, s],
+            recv_sem=recv_sem.at[p, s],
+            device_id=partner(axis, k),
+            device_id_type=pl.DeviceIdType.MESH,
+        )
+
+    def place(p):
+        spot = 0
+        for axis, k in plan(p, seq_count, dp_count):
+            if axis == "dp":
+                spot = 2 * spot + bit(me["dp"], k)
+        return spot
+
+    def spread(p, d):
+        return pltpu.make_async_remote_copy(
+            src_ref=gathered.at[p, place(p)],
+            dst_ref=gathered.at[p, place(p)],
+            send_sem=gather_send.at[p, d - 1],
+            recv_sem=gather_recv.at[p, d - 1],
+            device_id=dp_peer(d),
+            device_id_type=pl.DeviceIdType.MESH,
+        )
+
+    for wave in range(stages + PIECES + 1):
+        for p in range(PIECES):
+            s = wave - p
+            if s < 0 or s > stages + 1:
+                continue
+            if 0 < s <= stages:
+                exchange(p, s - 1).wait_recv()
+                axis, k = plan(p, seq_count, dp_count)[s - 1]
+                mine = half(source(s - 1), p, s - 1, bit(me[axis], k))
+                for b in range(got[s - 1].shape[1]):
+                    total = mine[b].astype(jnp.float32) + got[s - 1][p, b].astype(jnp.float32)
+                    if s < stages:
+                        kept[s - 1][p, b] = total.astype(jnp.bfloat16)
+                    else:
+                        gathered[p, place(p)] = total.astype(jnp.bfloat16)
+            if s < stages:
+                exchange(p, s).start()
+            elif s == stages:
+                for d in range(1, dp_count):
+                    spread(p, d).start()
+            else:
+                for d in range(1, dp_count):
+                    spread(p, d).wait_recv()
+                for c in range(dp_count):
+                    out_ref[p * rows : (p + 1) * rows, c * cols : (c + 1) * cols] = gathered[
+                        p, c
+                    ].astype(jnp.float32)
+    for p in range(PIECES):
+        for s in range(stages):
+            exchange(p, s).wait_send()
+        for d in range(1, dp_count):
+            spread(p, d).wait_send()
+
+
+def summed(part):
+    seq_count, dp_count = lax.axis_size("seq"), lax.axis_size("dp")
+    height, width = part.shape
+    share = height // seq_count
+    rows = share // PIECES
+    shapes = stage_shapes(seq_count, dp_count, rows, width)
+    low, dma = jnp.bfloat16, pltpu.SemaphoreType.DMA
+    return pl.pallas_call(
+        functools.partial(sum_kernel, seq_count, dp_count),
+        out_shape=shape(share, width, jnp.float32),
+        in_specs=[pl.BlockSpec(memory_space=pltpu.VMEM)],
+        out_specs=pl.BlockSpec(memory_space=pltpu.VMEM),
+        scratch_shapes=[pltpu.VMEM((PIECES, *s), low) for s in shapes]
+        + [pltpu.VMEM((PIECES, *s), low) for s in shapes[:-1]]
+        + [
+            pltpu.VMEM((PIECES, dp_count, rows, width // dp_count), low),
+            dma((PIECES, len(shapes))),
+            dma((PIECES, len(shapes))),
+            dma((PIECES, dp_count - 1)),
+            dma((PIECES, dp_count - 1)),
+        ],
+        compiler_params=pltpu.CompilerParams(
+            collective_id=0, has_side_effects=True, vmem_limit_bytes=40 * 2**20
+        ),
+        name="weight_sum",
+    )(part.reshape(seq_count // 2, 2, PIECES, rows, width))
 
 
 def params():
@@ -308,20 +469,20 @@
     )
     got_query2 = shifted(far_query2, stride)
     chain = (far_query1.astype(full) + got_query2.astype(full)).astype(low)
-    got_query = shifted(chain, stride)
-    query_grad = (own_query + got_query.astype(full)).astype(low)
+    weight_part = turned(fine, value_total).astype(low)
     back_rows = rows_by_rows(value_total, value_weight)
     row_grad = (key_sum.astype(full) + back_rows).astype(low)
-    return attended, query_grad, row_grad, value_total
+    chain, weight_part, row_grad = lax.optimization_barrier((chain, weight_part, row_grad))
+    got_query = shifted(chain, stride)
+    weight_grad = summed(weight_part)
+    query_grad = (own_query + got_query.astype(full)).astype(low)
+    return attended, query_grad, row_grad, weight_grad
 
 
 def shards(fine_rows, queries, value_weight, block_lists, out_grad):
-    attended, query_grad, row_grad, value_total = one_context(
+    attended, query_grad, row_grad, weight_grad = one_context(
         fine_rows[0], queries[0], value_weight, block_lists[0], out_grad[0]
     )
-    weight_part = turned(fine_rows[0], value_total).astype(jnp.bfloat16)
-    weight_share = lax.psum_scatter(weight_part, "seq", scatter_dimension=0, tiled=True)
-    weight_grad = lax.psum(weight_share.astype(jnp.float32), "dp")
     return attended[None], query_grad[None], row_grad[None], weight_grad
 
 

time: 365 us -> 241 us (0.66)
  waiting for transfers between devices: 113 us -> 52.5 us
  blocking collectives: 57.7 us -> 0 us
  between operations: 14.3 us -> 0.94 us
  Pallas kernels: 98.6 us -> 109 us
    pallas_call x0 -> x1, Pallas kernels: none -> 61.6 us  [summed(): pl.pallas_call(functools.partial(sum_kernel, seq_count, dp_count), out_sh...]
    psum x1 -> x0, blocking collectives: 57.7 us -> none  [shards(): weight_grad = lax.psum(weight_share.astype(jnp.float32), 'dp')]
    ppermute x12, waiting for transfers between devices: 103 us -> 52.5 us  [shifted(): return lax.ppermute(block, 'seq', route)]
    pallas_call x1, Pallas kernels: 31.7 us -> 17.5 us  [one_context(): pl.pallas_call(functools.partial(far_backward_kernel, scale=scale, count=...]
    pallas_call x1, Pallas kernels: 19.7 us -> 7.55 us  [one_context(): pl.pallas_call(functools.partial(own_forward_kernel, scale=scale), out_sh...]
    pallas_call x1, Pallas kernels: 17.4 us -> 6.94 us  [one_context(): pl.pallas_call(functools.partial(far_merge_kernel, scale=scale), out_shap...]
    unnamed x2 -> x0, waiting for transfers between devices: 9.17 us -> none
    pallas_call x1, Pallas kernels: 14.6 us -> 5.95 us  [one_context(): pl.pallas_call(functools.partial(far_first_kernel, scale=scale), out_shap...]
  transfers between devices with their start and end apart: 13 -> 12, of which waited for: 7 -> 4; matrix products, arithmetic and copies ran while one was open for 6% -> 15% of each run, Pallas kernels for 14% -> 36%
where the time goes in v2:
time: 241 us; the launch traced here: 240 us
  Pallas kernels  109 us (45%)
  waiting for transfers between devices  52.5 us (22%)
  starting transfers between devices  33.6 us (14%)
  matrix products  25.2 us (10%)
  local copies, waits for them, and re-layouts  15.4 us (6%)
  other arithmetic  3.33 us (1%)
    pallas_call x1, Pallas kernels, summed(): pl.pallas_call(functools.partial(sum_kernel, seq_count, dp_count), out_sh...  61.6 us
    ppermute x12, waiting for transfers between devices, shifted(): return lax.ppermute(block, 'seq', route)  52.5 us
    ppermute x12, starting transfers between devices, shifted(): return lax.ppermute(block, 'seq', route)  33.6 us
    pallas_call x1, Pallas kernels, one_context(): pl.pallas_call(functools.partial(far_backward_kernel, scale=scale, count=...  17.5 us
    pallas_call x1, Pallas kernels, one_context(): pl.pallas_call(functools.partial(own_backward_kernel, scale=scale), out_s...  9.39 us
    dot_general x1, matrix products, plain(): return jnp.dot(a, b, preferred_element_type=jnp.float32)  9.19 us
    dot_general x1, matrix products, rows_by_rows(): lax.dot_general(a, b, (((1,), (1,)), ((), ())), preferred_element_type=jn...  8.96 us
    unnamed x41, local copies, waits for them, and re-layouts  7.69 us
  transfers between devices with their start and end apart: 12, of which 4 were waited for; matrix products, arithmetic and copies ran while one was open for 15% of the time, Pallas kernels for 36%

profile of v2, /device:TPU:0, one launch (start us, length us, event | category | flops | bytes accessed | tf_op | source)
XLA Modules:
  0.0 239.9 jit_solution(16755031702961133094)
XLA Ops:
  0.6 1.3 collective-permute-start
  3.6 19.7 %collective-permute-done.q_ref.refs_0_ = bf16[256,1536]{1,0:T(8,128)(2,1)S(1)} collective-permute-done((bf16[256,1536]{1,0:T(8,128)(2,1)}, bf16[256,1536]{1,0:T(8,128)(2,1)S(1)}, u32[]{:S(2)}, u32[]{:S(2)}) %collective-permute-start) | collective-permute-done | bytes 786464 | tf_op jit(solution)/shard_map/ppermute | solution.py:23
  24.6 9.2 %convolution_convert_fusion.1.v_ref.refs_3_.refs_8_ = bf16[1024,1536]{1,0:T(8,128)(2,1)} fusion(bf16[1536,1536]{1,0:T(8,128)(2,1)} %param.7, bf16[1,1024,1536]{2,1,0:T(8,128)(2,1)} %param.5), kind=kOutput, calls=%fused_computation.3 | convolution fusion | flops 4833411072 | bytes 11010048 | tf_op jit(solution)/shard_map/dot_general | solution.py:35
  33.8 10.1 %collective-permute-done.1.q_ref.refs_5_ = bf16[256,1536]{1,0:T(8,128)(2,1)S(1)} collective-permute-done((bf16[256,1536]{1,0:T(8,128)(2,1)S(1)}, bf16[256,1536]{1,0:T(8,128)(2,1)S(1)}, u32[]{:S(2)}, u32[]{:S(2)}) %collective-permute-start.1) | collective-permute-done | bytes 786464 | tf_op jit(solution)/shard_map/ppermute | solution.py:23
  44.8 6.0 %far_first.1 = (bf16[256,1536]{1,0:T(8,128)(2,1)}, f32[256,128]{1,0:T(8,128)}) custom-call(s32[4]{0:T(128)} %clamp_reduce_fusion.index_ref, bf16[256,1536]{1,0:T(8,128)(2,1)} %copy-done.3, bf16[1024,1536]{1,0:T(8,128)(2,1)} %bitcast.22, bf16[1024,1536]{1,0:T(8,128)(2,1)} %convolution_convert_fusion.1.v_ref.refs_3_.refs_8_), custom_call_target="tpu_custom_call" | custom-call | flops 201326592 | bytes 3145728 | tf_op jit(solution)/shard_map/far_first/pallas_call | solution.py:379
  50.8 3.4 %collective-permute-start.2 = (bf16[256,1536]{1,0:T(8,128)(2,1)}, bf16[256,1536]{1,0:T(8,128)(2,1)S(1)}, u32[]{:S(2)}, u32[]{:S(2)}) collective-permute-start(bf16[256,1536]{1,0:T(8,128)(2,1)} %get-tuple-element.23), channel_id=1, source_target_pairs={{0,2},{1,3},{2,4},{3,5},{4,6},{5,7},{8,10},{9,11},{10,12},{11,13},... | collective-permute-start | bytes 2359304 | tf_op jit(solution)/shard_map/ppermute | solution.py:23
  54.1 1.3 collective-permute-start.6
  55.4 4.6 %collective-permute-start.3 = (f32[256,128]{1,0:T(8,128)}, f32[256,128]{1,0:T(8,128)S(1)}, u32[]{:S(2)}, u32[]{:S(2)}) collective-permute-start(f32[256,128]{1,0:T(8,128)} %get-tuple-element.24), channel_id=1, source_target_pairs={{0,2},{1,3},{2,4},{3,5},{4,6},{5,7},{8,10},{9,11},{10,12},{11,13},... | collective-permute-start | bytes 393224 | tf_op jit(solution)/shard_map/ppermute | solution.py:23
  60.8 11.4 %collective-permute-done.3.got_stat_ref = f32[256,128]{1,0:T(8,128)S(1)} collective-permute-done((f32[256,128]{1,0:T(8,128)}, f32[256,128]{1,0:T(8,128)S(1)}, u32[]{:S(2)}, u32[]{:S(2)}) %collective-permute-start.3) | collective-permute-done | bytes 131104 | tf_op jit(solution)/shard_map/ppermute | solution.py:23
  73.1 6.9 %far_merge.1 = (bf16[256,1536]{1,0:T(8,128)(2,1)}, f32[256,128]{1,0:T(8,128)}) custom-call(s32[4]{0:T(128)} %clamp_reduce_fusion.1.index_ref, s32[1]{0:T(128)} %bitcast.live_ref, bf16[256,1536]{1,0:T(8,128)(2,1)} %copy-done.2, bf16[1024,1536]{1,0:T(8,128)(2,1)} %bitcast.23, bf16[1024,1536]{1,0:T(8,128)(2,1)} %convolution_convert_fusion.1.v_ref.refs_3_.refs_8_, ...), custom_call_target="tpu_custom_call" | custom-call | flops 201326592 | bytes 3932160 | tf_op jit(solution)/shard_map/far_merge/pallas_call | solution.py:393
  80.1 4.3 %collective-permute-start.4 = (bf16[256,1536]{1,0:T(8,128)(2,1)}, bf16[256,1536]{1,0:T(8,128)(2,1)S(1)}, u32[]{:S(2)}, u32[]{:S(2)}) collective-permute-start(bf16[256,1536]{1,0:T(8,128)(2,1)} %get-tuple-element.25), channel_id=1, source_target_pairs={{0,2},{1,3},{2,4},{3,5},{4,6},{5,7},{8,10},{9,11},{10,12},{11,13},... | collective-permute-start | bytes 2359304 | tf_op jit(solution)/shard_map/ppermute | solution.py:23
  84.4 1.3 collective-permute-start.8
  85.7 4.6 %collective-permute-start.5 = (f32[256,128]{1,0:T(8,128)}, f32[256,128]{1,0:T(8,128)S(1)}, u32[]{:S(2)}, u32[]{:S(2)}) collective-permute-start(f32[256,128]{1,0:T(8,128)} %get-tuple-element.26), channel_id=1, source_target_pairs={{0,2},{1,3},{2,4},{3,5},{4,6},{5,7},{8,10},{9,11},{10,12},{11,13},... | collective-permute-start | bytes 393224 | tf_op jit(solution)/shard_map/ppermute | solution.py:23
  90.3 11.2 %collective-permute-done.5.got_stat_ref = f32[256,128]{1,0:T(8,128)S(1)} collective-permute-done((f32[256,128]{1,0:T(8,128)}, f32[256,128]{1,0:T(8,128)S(1)}, u32[]{:S(2)}, u32[]{:S(2)}) %collective-permute-start.5) | collective-permute-done | bytes 131104 | tf_op jit(solution)/shard_map/ppermute | solution.py:23
  103.1 7.6 %own_forward.1 = (bf16[256,1536]{1,0:T(8,128)(2,1)}, f32[256,128]{1,0:T(8,128)}) custom-call(s32[1]{0:T(128)} %bitcast.live_ref, bf16[256,1536]{1,0:T(8,128)(2,1)} %bitcast.29, bf16[256,1536]{1,0:T(8,128)(2,1)} %bitcast.31, bf16[1024,1536]{1,0:T(8,128)(2,1)} %bitcast.24, bf16[1024,1536]{1,0:T(8,128)(2,1)} %convolution_convert_fusion.1.v_ref.refs_3_.refs_8_, ...), custom_call_target="tpu_custom_call" | custom-call | flops 402653184 | bytes 9437184 | tf_op jit(solution)/shard_map/own_forward/pallas_call | solution.py:407
  113.9 9.4 %own_backward.1 = (f32[256,1536]{1,0:T(8,128)}, bf16[1024,1536]{1,0:T(8,128)(2,1)}, bf16[1024,1536]{1,0:T(8,128)(2,1)}) custom-call(bf16[256,1536]{1,0:T(8,128)(2,1)} %bitcast.30, bf16[256,1536]{1,0:T(8,128)(2,1)} %bitcast.32, bf16[1024,1536]{1,0:T(8,128)(2,1)} %bitcast.25, bf16[1024,1536]{1,0:T(8,128)(2,1)} %convolution_convert_fusion.1.v_ref.refs_3_.refs_8_, ...), custom_call_target="tpu_custom_call" | custom-call | flops 1006632960 | bytes 15728640 | tf_op jit(solution)/shard_map/own_backward/pallas_call | solution.py:422
  124.3 17.5 %far_backward.1 = (bf16[256,1536]{1,0:T(8,128)(2,1)}, bf16[256,1536]{1,0:T(8,128)(2,1)}, bf16[1024,1536]{1,0:T(8,128)(2,1)}, bf16[1024,1536]{1,0:T(8,128)(2,1)}) custom-call(s32[8]{0:T(128)} %pad_add_fusion.index_ref, bf16[256,1536]{1,0:T(8,128)(2,1)} %copy-done.2, bf16[256,1536]{1,0:T(8,128)(2,1)} %copy-done.6, bf16[1024,1536]{1,0:T(8,128)(2,1)} %bitcast.26, ...), custom_call_target="tpu_custom_call" | custom-call | flops 1006632960 | bytes 19660800 | tf_op jit(solution)/shard_map/far_backward/pallas_call | solution.py:441
  141.8 5.1 %collective-permute-start.10 = (bf16[256,1536]{1,0:T(8,128)(2,1)}, bf16[256,1536]{1,0:T(8,128)(2,1)S(1)}, u32[]{:S(2)}, u32[]{:S(2)}) collective-permute-start(bf16[256,1536]{1,0:T(8,128)(2,1)} %get-tuple-element.34), channel_id=1, source_target_pairs={{0,2},{1,3},{2,4},{3,5},{4,6},{5,7},{8,10},{9,11},{10,12},{11,13},... | collective-permute-start | bytes 2359304 | tf_op jit(solution)/shard_map/ppermute | solution.py:23
  147.0 9.0 %add_convert_fusion = bf16[1024,1536]{1,0:T(8,128)(2,1)} fusion(bf16[1024,1536]{1,0:T(8,128)(2,1)} %get-tuple-element.36, bf16[1024,1536]{1,0:T(8,128)(2,1)} %get-tuple-element.35, bf16[1536,1536]{1,0:T(8,128)(2,1)S(1)} %bitcast.37), kind=kOutput, calls=%fused_computation.2 | convolution fusion | flops 4836556800 | bytes 14155776 | tf_op jit(solution)/shard_map/dot_general | solution.py:27
  156.0 7.0 %fusion = bf16[1536,1536]{0,1:T(8,128)(2,1)} fusion(bf16[1024,1536]{1,0:T(8,128)(2,1)S(1)} %copy-done.17, bf16[1,1024,1536]{2,1,0:T(8,128)(2,1)S(1)} %copy-done.1), kind=kOutput, calls=%fused_computation.1 | convolution fusion | flops 4834197504 | bytes 11010048 | tf_op jit(solution)/shard_map/dot_general | solution.py:31
  163.3 3.9 %collective-permute-start.11 = (bf16[256,1536]{1,0:T(8,128)(2,1)S(1)}, bf16[256,1536]{1,0:T(8,128)(2,1)S(1)}, u32[]{:S(2)}, u32[]{:S(2)}) collective-permute-start(bf16[256,1536]{1,0:T(8,128)(2,1)S(1)} %add_convert_fusion.2), channel_id=1, source_target_pairs={{0,2},{1,3},{2,4},{3,5},{4,6},{5,7},{8,10},{9,11},{10,12},{11,13},... | collective-permute-start | bytes 2359304 | tf_op jit(solution)/shard_map/ppermute | solution.py:23
  167.2 6.6 %copy.14 = bf16[1536,1536]{1,0:T(8,128)(2,1)} copy(bf16[1536,1536]{0,1:T(8,128)(2,1)} %fusion) | data formatting | bytes 9437184 | tf_op jit(solution)/shard_map/optimization_barrier | solution.py:475
  173.8 2.3 copy-done
  176.2 61.6 %weight_sum.1 = f32[192,1536]{1,0:T(8,128)S(1)} custom-call(bf16[4,2,3,64,1536]{4,3,2,1,0:T(8,128)(2,1)S(1)} %bitcast.21), custom_call_target="tpu_custom_call" | custom-call | tf_op jit(solution)/shard_map/weight_sum/pallas_call | solution.py:312
  (60 shorter events, 13.6 us)
Async XLA Ops:
  0.6 22.7 %collective-permute-start = (bf16[256,1536]{1,0:T(8,128)(2,1)}, bf16[256,1536]{1,0:T(8,128)(2,1)S(1)}, u32[]{:S(2)}, u32[]{:S(2)}) collective-permute-start(bf16[256,1536]{1,0:T(8,128)(2,1)} %bitcast.28), channel_id=1, source_target_pairs={{2,0},{3,1},{4,2},{5,3},{6,4},{7,5},{10,8},{11,9},{12,10},{13,11},... | collective-permute-start | bytes 2359304 | tf_op jit(solution)/shard_map/ppermute | solution.py:23
  23.3 10.5 %copy-start.2 = (bf16[256,1536]{1,0:T(8,128)(2,1)}, bf16[256,1536]{1,0:T(8,128)(2,1)S(1)}, u32[]{:S(2)}) copy-start(bf16[256,1536]{1,0:T(8,128)(2,1)S(1)} %collective-permute-done.q_ref.refs_0_) | copy-start | bytes 2359300
  23.3 20.6 %collective-permute-start.1 = (bf16[256,1536]{1,0:T(8,128)(2,1)S(1)}, bf16[256,1536]{1,0:T(8,128)(2,1)S(1)}, u32[]{:S(2)}, u32[]{:S(2)}) collective-permute-start(bf16[256,1536]{1,0:T(8,128)(2,1)S(1)} %collective-permute-done.q_ref.refs_0_), channel_id=1, source_target_pairs={{2,0},{3,1},{4,2},{5,3},{6,4},{7,5},{10,8},{11,9},{12,10},{13,11},... | collective-permute-start | bytes 2359304 | tf_op jit(solution)/shard_map/ppermute | solution.py:23
  44.8 9.3 %copy-start.4 = (bf16[1,256,1536]{2,1,0:T(8,128)(2,1)S(1)}, bf16[1,256,1536]{2,1,0:T(8,128)(2,1)}, u32[]{:S(2)}) copy-start(bf16[1,256,1536]{2,1,0:T(8,128)(2,1)} %param.9) | copy-start | bytes 2359300
  50.8 21.4 %collective-permute-start.2 = (bf16[256,1536]{1,0:T(8,128)(2,1)}, bf16[256,1536]{1,0:T(8,128)(2,1)S(1)}, u32[]{:S(2)}, u32[]{:S(2)}) collective-permute-start(bf16[256,1536]{1,0:T(8,128)(2,1)} %get-tuple-element.23), channel_id=1, source_target_pairs={{0,2},{1,3},{2,4},{3,5},{4,6},{5,7},{8,10},{9,11},{10,12},{11,13},... | collective-permute-start | bytes 2359304 | tf_op jit(solution)/shard_map/ppermute | solution.py:23
  54.1 30.2 %collective-permute-start.6 = (bf16[256,1536]{1,0:T(8,128)(2,1)S(1)}, bf16[256,1536]{1,0:T(8,128)(2,1)S(1)}, u32[]{:S(2)}, u32[]{:S(2)}) collective-permute-start(bf16[256,1536]{1,0:T(8,128)(2,1)S(1)} %bitcast.33), channel_id=1, source_target_pairs={{2,0},{3,1},{4,2},{5,3},{6,4},{7,5},{10,8},{11,9},{12,10},{13,11},... | collective-permute-start | bytes 2359304 | tf_op jit(solution)/shard_map/ppermute | solution.py:23
  55.4 16.8 %collective-permute-start.3 = (f32[256,128]{1,0:T(8,128)}, f32[256,128]{1,0:T(8,128)S(1)}, u32[]{:S(2)}, u32[]{:S(2)}) collective-permute-start(f32[256,128]{1,0:T(8,128)} %get-tuple-element.24), channel_id=1, source_target_pairs={{0,2},{1,3},{2,4},{3,5},{4,6},{5,7},{8,10},{9,11},{10,12},{11,13},... | collective-permute-start | bytes 393224 | tf_op jit(solution)/shard_map/ppermute | solution.py:23
  80.1 21.5 %collective-permute-start.4 = (bf16[256,1536]{1,0:T(8,128)(2,1)}, bf16[256,1536]{1,0:T(8,128)(2,1)S(1)}, u32[]{:S(2)}, u32[]{:S(2)}) collective-permute-start(bf16[256,1536]{1,0:T(8,128)(2,1)} %get-tuple-element.25), channel_id=1, source_target_pairs={{0,2},{1,3},{2,4},{3,5},{4,6},{5,7},{8,10},{9,11},{10,12},{11,13},... | collective-permute-start | bytes 2359304 | tf_op jit(solution)/shard_map/ppermute | solution.py:23
  84.4 26.3 %copy-start.6 = (bf16[256,1536]{1,0:T(8,128)(2,1)}, bf16[256,1536]{1,0:T(8,128)(2,1)S(1)}, u32[]{:S(2)}) copy-start(bf16[256,1536]{1,0:T(8,128)(2,1)S(1)} %collective-permute-done.6.refs_1_) | copy-start | bytes 2359300
  84.4 38.9 %collective-permute-start.8 = (bf16[256,1536]{1,0:T(8,128)(2,1)S(1)}, bf16[256,1536]{1,0:T(8,128)(2,1)S(1)}, u32[]{:S(2)}, u32[]{:S(2)}) collective-permute-start(bf16[256,1536]{1,0:T(8,128)(2,1)S(1)} %collective-permute-done.6.refs_1_), channel_id=1, source_target_pairs={{2,0},{3,1},{4,2},{5,3},{6,4},{7,5},{10,8},{11,9},{12,10},{13,11},... | collective-permute-start | bytes 2359304 | tf_op jit(solution)/shard_map/ppermute | solution.py:23
  85.7 27.6 %copy-start.15 = (s32[4]{0:T(128)S(1)}, s32[4]{0:T(128)}, u32[]{:S(2)}) copy-start(s32[4]{0:T(128)} %clamp_reduce_fusion.index_ref) | copy-start | bytes 52
  85.7 27.6 %copy-start.16 = (s32[4]{0:T(128)S(1)}, s32[4]{0:T(128)}, u32[]{:S(2)}) copy-start(s32[4]{0:T(128)} %clamp_reduce_fusion.1.index_ref) | copy-start | bytes 52
  85.7 15.8 %collective-permute-start.5 = (f32[256,128]{1,0:T(8,128)}, f32[256,128]{1,0:T(8,128)S(1)}, u32[]{:S(2)}, u32[]{:S(2)}) collective-permute-start(f32[256,128]{1,0:T(8,128)} %get-tuple-element.26), channel_id=1, source_target_pairs={{0,2},{1,3},{2,4},{3,5},{4,6},{5,7},{8,10},{9,11},{10,12},{11,13},... | collective-permute-start | bytes 393224 | tf_op jit(solution)/shard_map/ppermute | solution.py:23
  110.6 12.7 %collective-permute-start.9 = (f32[256,128]{1,0:T(8,128)}, f32[256,128]{1,0:T(8,128)S(1)}, u32[]{:S(2)}, u32[]{:S(2)}) collective-permute-start(f32[256,128]{1,0:T(8,128)} %get-tuple-element.28.stat_ref), channel_id=1, source_target_pairs={{4,0},{5,1},{6,2},{7,3},{12,8},{13,9},{14,10},{15,11},{20,16},{21,... | collective-permute-start | bytes 393224 | tf_op jit(solution)/shard_map/ppermute | solution.py:23
  111.9 11.4 %collective-permute-start.7 = (f32[256,128]{1,0:T(8,128)}, f32[256,128]{1,0:T(8,128)S(1)}, u32[]{:S(2)}, u32[]{:S(2)}) collective-permute-start(f32[256,128]{1,0:T(8,128)} %get-tuple-element.28.stat_ref), channel_id=1, source_target_pairs={{2,0},{3,1},{4,2},{5,3},{6,4},{7,5},{10,8},{11,9},{12,10},{13,11},... | collective-permute-start | bytes 393224 | tf_op jit(solution)/shard_map/ppermute | solution.py:23
  113.9 33.1 %slice-start = ((s8[4718592]{0:T(1024)(128)(4,1)}), s8[524288]{0:T(1024)(128)(4,1)S(1)}, s32[]{:S(2)}) async-start(s8[4718592]{0:T(1024)(128)(4,1)} %bitcast.36), calls=%async_computation | async-start | bytes 1048576
  124.3 22.7 %slice-start.1 = ((s8[4718592]{0:T(1024)(128)(4,1)}), s8[4194304]{0:T(1024)(128)(4,1)S(1)}, s32[]{:S(2)}) async-start(s8[4718592]{0:T(1024)(128)(4,1)} %bitcast.36), calls=%async_computation.1 | async-start | bytes 8388608
  141.8 21.2 %collective-permute-start.10 = (bf16[256,1536]{1,0:T(8,128)(2,1)}, bf16[256,1536]{1,0:T(8,128)(2,1)S(1)}, u32[]{:S(2)}, u32[]{:S(2)}) collective-permute-start(bf16[256,1536]{1,0:T(8,128)(2,1)} %get-tuple-element.34), channel_id=1, source_target_pairs={{0,2},{1,3},{2,4},{3,5},{4,6},{5,7},{8,10},{9,11},{10,12},{11,13},... | collective-permute-start | bytes 2359304 | tf_op jit(solution)/shard_map/ppermute | solution.py:23
  147.0 9.0 %copy-start.1 = (bf16[1,1024,1536]{2,1,0:T(8,128)(2,1)S(1)}, bf16[1,1024,1536]{2,1,0:T(8,128)(2,1)}, u32[]{:S(2)}) copy-start(bf16[1,1024,1536]{2,1,0:T(8,128)(2,1)} %param.5) | copy-start | bytes 9437188
  147.0 9.0 %copy-start.17 = (bf16[1024,1536]{1,0:T(8,128)(2,1)S(1)}, bf16[1024,1536]{1,0:T(8,128)(2,1)}, u32[]{:S(2)}) copy-start(bf16[1024,1536]{1,0:T(8,128)(2,1)} %get-tuple-element.35) | copy-start | bytes 9437188
  156.0 7.1 %copy-start.10 = (bf16[256,1536]{1,0:T(8,128)(2,1)S(1)}, bf16[256,1536]{1,0:T(8,128)(2,1)}, u32[]{:S(2)}) copy-start(bf16[256,1536]{1,0:T(8,128)(2,1)} %get-tuple-element.33) | copy-start | bytes 2359300
  163.3 74.5 %collective-permute-start.11 = (bf16[256,1536]{1,0:T(8,128)(2,1)S(1)}, bf16[256,1536]{1,0:T(8,128)(2,1)S(1)}, u32[]{:S(2)}, u32[]{:S(2)}) collective-permute-start(bf16[256,1536]{1,0:T(8,128)(2,1)S(1)} %add_convert_fusion.2), channel_id=1, source_target_pairs={{0,2},{1,3},{2,4},{3,5},{4,6},{5,7},{8,10},{9,11},{10,12},{11,13},... | collective-permute-start | bytes 2359304 | tf_op jit(solution)/shard_map/ppermute | solution.py:23
  173.8 2.3 copy-start
  176.2 61.6 %copy-start.5 = (f32[256,1536]{1,0:T(8,128)S(1)}, f32[256,1536]{1,0:T(8,128)}, u32[]{:S(2)}) copy-start(f32[256,1536]{1,0:T(8,128)} %get-tuple-element.29) | copy-start | bytes 4718596
  (8 other events, 6.8 us)
